TPU v7x, 512 devices: a whole 4x4x16 slice. The times are simulated.
512 devices in a mesh: dom: 4 (over z_lo), seq: 32 (over x, y, core), rep: 4 (over z_hi).
Axes of the slice: x: 4, y: 4, z: 16 (z_hi: 4, z_lo: 4; z = z_hi * 4 + z_lo), core: 2. Of those that a mesh axis runs over, the one named last changes fastest.
Arguments:
- counts: int32 [32], P('rep'), parts along dimension 0, may hold values from 0 to 4, as said below
- video_query: bfloat16 [32, 1536, 2048], P(('rep', 'dom'), 'seq'), parts along dimension 0, may hold values from -21 to 21
- video_key: bfloat16 [32, 1536, 2048], P(('rep', 'dom'), 'seq'), parts along dimension 0, may hold values from -10.2 to 10.2
- video_value: bfloat16 [32, 1536, 2048], P(('rep', 'dom'), 'seq'), parts along dimension 0, may hold values from -6 to 6
- text_query: bfloat16 [32, 256, 2048], P(('rep', 'dom'), 'seq'), parts along dimension 0, may hold values from -6 to 6
- text_key: bfloat16 [32, 256, 2048], P(('rep', 'dom'), 'seq'), parts along dimension 0, may hold values from -6 to 6
- text_value: bfloat16 [32, 256, 2048], P(('rep', 'dom'), 'seq'), parts along dimension 0, may hold values from -6 to 6
- fresh_noise: bfloat16 [32, 1536, 2048], P(('rep', 'dom'), 'seq'), parts along dimension 0, may hold values from -6 to 6
Outputs:
- video_out: bfloat16 [32, 1536, 2048], P(('rep', 'dom'), 'seq'), parts along dimension 0
- text_out: bfloat16 [32, 256, 2048], P(('rep', 'dom'), 'seq'), parts along dimension 0
There are 4 independent parts, one for each index of `rep`. A program takes and returns all parts, laid end to end along the dimension named above; each array names one. Nothing has to cross between parts.
Inputs may be any that keep to these rules, and one draw needn't show every extreme that they name: counts sum to 8; some particle has exactly 4 offspring; particles 0 to 1 together have more than 4 offspring.
All inputs are finite; a program needn't handle non-finite values.
Results may differ from a plain program's by a relative error of at most 0.005.
Values may be sent and summed in bfloat16 or wider, within the bound.
No kernel may reach another device: no remote copies, remote signals or barrier semaphores. Data moves between devices by JAX's collectives and lax.ppermute only.
A program may use at most 64 MiB of HBM per device.

v0:
```python
import jax
import jax.numpy as jnp
from jax import lax
from jax.sharding import PartitionSpec as P

HEADS = 16


def ancestors(counts):
    running = jnp.cumsum(counts)
    slot_ids = jnp.arange(counts.shape[0], dtype=jnp.int32)
    return jnp.sum((running[None, :] <= slot_ids[:, None]).astype(jnp.int32), axis=1)


def attend(queries, key_rows, value_rows):
    scores = lax.dot_general(
        queries, key_rows, (((1,), (1,)), ((), ())), preferred_element_type=jnp.float32
    )
    scores = scores * queries.shape[1] ** (-0.5)
    row_max = jnp.max(scores, axis=1, keepdims=True)
    weights = jnp.exp(scores - row_max)
    row_sum = jnp.sum(weights, axis=1, keepdims=True)
    rounded = (weights / row_sum).astype(jnp.bfloat16)
    return jnp.dot(rounded, value_rows, preferred_element_type=jnp.float32).astype(jnp.bfloat16)


def attend_one(queries, key_rows, value_rows):
    row_count = queries.shape[0]
    block_rows = min(512, row_count)
    block_count = -(-row_count // block_rows)
    padded = jnp.pad(queries, ((0, block_count * block_rows - row_count), (0, 0)))
    blocks = padded.reshape(block_count, block_rows, queries.shape[1])

    def one_block(query_block):
        return attend(query_block, key_rows, value_rows)

    result = lax.map(one_block, blocks)
    return result.reshape(block_count * block_rows, queries.shape[1])[:row_count]


def attend_items(pieces):
    queries, key_rows, value_rows = pieces

    def single(member):
        return attend_one(member[0], member[1], member[2])

    return lax.map(single, (queries[0], key_rows[0], value_rows[0]))[None]


def head_layout(video_part, text_part, features):
    joined = jnp.concatenate([video_part, text_part], axis=1)
    resident = joined.shape[0]
    row_count = joined.shape[1]
    split_heads = joined.reshape(resident, row_count, HEADS, features // HEADS).transpose(
        0, 2, 1, 3
    )
    devices = lax.axis_size("seq")
    return split_heads.reshape(devices, resident * HEADS // devices, row_count, features // HEADS)


def token_layout(attended, resident, features):
    returned = lax.all_to_all(attended, "seq", split_axis=2, concat_axis=0, tiled=True)
    row_count = returned.shape[2]
    returned = returned.reshape(resident, HEADS, row_count, features // HEADS).transpose(0, 2, 1, 3)
    return returned.reshape(resident, row_count, features)


def per_device(
    counts, video_query, video_key, video_value, text_query, text_key, text_value, fresh_noise
):
    resident = video_query.shape[0]
    video_rows = video_query.shape[1]
    features = video_query.shape[2]
    lineage = ancestors(counts)
    chosen = lax.dynamic_slice_in_dim(lineage, lax.axis_index("dom") * resident, resident)
    copies = (
        lax.all_gather(video_query, "dom", axis=0, tiled=True),
        lax.all_gather(video_key, "dom", axis=0, tiled=True),
        lax.all_gather(video_value, "dom", axis=0, tiled=True),
        lax.all_gather(text_query, "dom", axis=0, tiled=True),
        lax.all_gather(text_key, "dom", axis=0, tiled=True),
        lax.all_gather(text_value, "dom", axis=0, tiled=True),
    )
    picked = [jnp.take(whole, chosen, axis=0) for whole in copies]
    query_heads = head_layout(picked[0], picked[3], features)
    key_heads = head_layout(picked[1], picked[4], features)
    value_heads = head_layout(picked[2], picked[5], features)
    attended = attend_items(
        (
            lax.all_to_all(query_heads, "seq", split_axis=0, concat_axis=2, tiled=True),
            lax.all_to_all(key_heads, "seq", split_axis=0, concat_axis=2, tiled=True),
            lax.all_to_all(value_heads, "seq", split_axis=0, concat_axis=2, tiled=True),
        )
    )
    mixed = token_layout(attended, resident, features)
    video_out = (
        mixed[:, :video_rows].astype(jnp.float32) + fresh_noise.astype(jnp.float32)
    ).astype(jnp.bfloat16)
    return (video_out, mixed[:, video_rows:])


def solution(mesh):
    placed = (
        P("rep"),
        P(("rep", "dom"), "seq", None),
        P(("rep", "dom"), "seq", None),
        P(("rep", "dom"), "seq", None),
        P(("rep", "dom"), "seq", None),
        P(("rep", "dom"), "seq", None),
        P(("rep", "dom"), "seq", None),
        P(("rep", "dom"), "seq", None),
    )
    return jax.shard_map(
        per_device,
        mesh=mesh,
        in_specs=placed,
        out_specs=(P(("rep", "dom"), "seq", None), P(("rep", "dom"), "seq", None)),
        check_vma=False,
    )
```

profile of v0, /device:TPU:1, one launch (start us, length us, event | category | flops | bytes accessed | tf_op | source)
XLA Modules:
  0.0 267.3 jit_solution(2722595735888443296)
XLA Ops:
  10.2 13.8 %all_gather.23 = bf16[8,8,2048]{2,1,0:T(8,128)(2,1)S(1)} all-gather(bf16[2,8,2048]{2,1,0:T(8,128)(2,1)} %param.20), channel_id=1, replica_groups=mesh['dom'=4,'seq'=32,'rep'=4] {'dom'}, dimensions={0}, use_global_device_ids=true | all-gather | bytes 327680 | tf_op jit(solution)/shard_map/all_gather | solution.py:82
  24.8 11.9 %all_gather.19 = bf16[8,8,2048]{2,1,0:T(8,128)(2,1)S(1)} all-gather(bf16[2,8,2048]{2,1,0:T(8,128)(2,1)} %param.18), channel_id=1, replica_groups=mesh['dom'=4,'seq'=32,'rep'=4] {'dom'}, dimensions={0}, use_global_device_ids=true | all-gather | bytes 327680 | tf_op jit(solution)/shard_map/all_gather | solution.py:80
  37.3 15.0 %all_gather.21 = bf16[8,8,2048]{2,1,0:T(8,128)(2,1)S(1)} all-gather(bf16[2,8,2048]{2,1,0:T(8,128)(2,1)} %param.19), channel_id=1, replica_groups=mesh['dom'=4,'seq'=32,'rep'=4] {'dom'}, dimensions={0}, use_global_device_ids=true | all-gather | bytes 327680 | tf_op jit(solution)/shard_map/all_gather | solution.py:81
  53.0 15.4 %all-gather.8.cloned.1.call-done = bf16[8,48,2048]{2,1,0:T(8,128)(2,1)} async-done(((bf16[2,48,2048]{2,1,0:T(8,128)(2,1)}), bf16[8,48,2048]{2,1,0:T(8,128)(2,1)}) %all-gather.8.cloned.1.call-update) | async-done | bytes 1572880 | tf_op jit(solution)/shard_map/all_gather | solution.py:79
  68.4 2.0 gather_fusion.4
  70.3 46.8 %all-gather.4.cloned.1.call-done = bf16[8,48,2048]{2,1,0:T(8,128)(2,1)} async-done(((bf16[2,48,2048]{2,1,0:T(8,128)(2,1)}), bf16[8,48,2048]{2,1,0:T(8,128)(2,1)}) %all-gather.4.cloned.1.call-update) | async-done | bytes 1572880 | tf_op jit(solution)/shard_map/all_gather | solution.py:77
  117.1 2.0 gather_fusion
  119.1 46.4 %all-gather.6.cloned.1.call-done = bf16[8,48,2048]{2,1,0:T(8,128)(2,1)} async-done(((bf16[2,48,2048]{2,1,0:T(8,128)(2,1)}), bf16[8,48,2048]{2,1,0:T(8,128)(2,1)}) %all-gather.6.cloned.1.call-update) | async-done | bytes 1572880 | tf_op jit(solution)/shard_map/all_gather | solution.py:78
  165.6 2.0 gather_fusion.2
  167.9 0.9 copy.29
  168.8 7.8 %all-to-all-start = ((bf16[32,1,56,128]{3,2,1,0:T(8,128)(2,1)}), bf16[32,1,56,128]{3,2,1,0:T(8,128)(2,1)S(1)}, u32[]{:S(2)}, u32[]{:S(2)}) async-start(bf16[32,1,56,128]{3,2,1,0:T(8,128)(2,1)} %bitcast.6), calls=%async_computation | async-start | bytes 917504 | tf_op jit(solution)/shard_map/all_to_all | solution.py:90
  177.6 10.0 %all-to-all-done = bf16[32,1,56,128]{3,2,1,0:T(8,128)(2,1)S(1)} async-done(((bf16[32,1,56,128]{3,2,1,0:T(8,128)(2,1)}), bf16[32,1,56,128]{3,2,1,0:T(8,128)(2,1)S(1)}, u32[]{:S(2)}, u32[]{:S(2)}) %all-to-all-start) | async-done | bytes 458784 | tf_op jit(solution)/shard_map/all_to_all | solution.py:90
  187.5 3.7 %all-to-all-start.1 = ((bf16[32,1,56,128]{3,2,1,0:T(8,128)(2,1)}), bf16[32,1,56,128]{3,2,1,0:T(8,128)(2,1)S(1)}, u32[]{:S(2)}, u32[]{:S(2)}) async-start(bf16[32,1,56,128]{3,2,1,0:T(8,128)(2,1)} %bitcast.10), calls=%async_computation.1 | async-start | bytes 917504 | tf_op jit(solution)/shard_map/all_to_all | solution.py:91
  192.3 9.8 %all-to-all-done.1 = bf16[32,1,56,128]{3,2,1,0:T(8,128)(2,1)S(1)} async-done(((bf16[32,1,56,128]{3,2,1,0:T(8,128)(2,1)}), bf16[32,1,56,128]{3,2,1,0:T(8,128)(2,1)S(1)}, u32[]{:S(2)}, u32[]{:S(2)}) %all-to-all-start.1) | async-done | bytes 458784 | tf_op jit(solution)/shard_map/all_to_all | solution.py:91
  202.1 3.9 %all-to-all-start.2 = ((bf16[32,1,56,128]{3,2,1,0:T(8,128)(2,1)}), bf16[32,1,56,128]{3,2,1,0:T(8,128)(2,1)S(1)}, u32[]{:S(2)}, u32[]{:S(2)}) async-start(bf16[32,1,56,128]{3,2,1,0:T(8,128)(2,1)} %bitcast.13), calls=%async_computation.2 | async-start | bytes 917504 | tf_op jit(solution)/shard_map/all_to_all | solution.py:92
  206.0 10.6 %all-to-all-done.2 = bf16[32,1,56,128]{3,2,1,0:T(8,128)(2,1)S(1)} async-done(((bf16[32,1,56,128]{3,2,1,0:T(8,128)(2,1)}), bf16[32,1,56,128]{3,2,1,0:T(8,128)(2,1)S(1)}, u32[]{:S(2)}, u32[]{:S(2)}) %all-to-all-start.2) | async-done | bytes 458784 | tf_op jit(solution)/shard_map/all_to_all | solution.py:92
  216.7 9.7 %while.17 = (s32[]{:T(128)}, bf16[4,512,128]{2,1,0:T(8,128)(2,1)S(1)}, bf16[4,512,128]{2,1,0:T(8,128)(2,1)S(1)}, bf16[1792,128]{1,0:T(8,128)(2,1)S(1)}, bf16[1792,128]{1,0:T(8,128)(2,1)S(1)}, /*index=5*/s32[]{:T(128)}) while((s32[]{:T(128)}, bf16[4,512,128]{2,1,0:T(8,128)(2,1)S(1)}, bf16[4,512,128]{2,1,0:T(8,128)(2,1)S(1)}, ...), condition=%wide.region_5.8_spmd, body=%wide.region_2.7_spmd.sunk | while | flops 478084096 | bytes 12200013 | solution.py:37
  218.1 1.0 fusion.19
  220.6 1.0 fusion.19
  223.0 1.0 fusion.19
  225.4 1.0 fusion.19
  226.4 7.1 %copy.43 = bf16[1,1,1792,128]{3,1,0,2:T(2,128)(2,1)S(1)} copy(bf16[1,1,1792,128]{3,2,1,0:T(8,128)(2,1)S(1)} %slice_bitcast_fusion) | data formatting | bytes 917504 | tf_op jit(solution)/shard_map/broadcast_in_dim | solution.py:47
  234.1 10.2 %reduce = bf16[1792,128]{1,0:T(8,128)(2,1)S(1)} reduce(bf16[1792,1,1,128]{3,2,1,0:T(2,128)(2,1)S(1)} %bitcast.69, bf16[]{:T(256)} %broadcast.98), dimensions={1,2}, to_apply=%bitcast.56.reduce_sub_computation | reduce | bytes 917506
  244.4 14.3 %all_to_all.16 = bf16[32,2,3584]{2,1,0:T(2,128)(2,1)S(1)} all-to-all(bf16[32,2,3584]{2,1,0:T(2,128)(2,1)S(1)} %reshape.170), channel_id=1, replica_groups=mesh['dom'=4,'seq'=32,'rep'=4] {'seq'}, dimensions={0} | all-to-all | bytes 917504 | tf_op jit(solution)/shard_map/all_to_all | solution.py:62
  (45 shorter events, 15.9 us)
Async XLA Ops:
  7.2 61.2 %all-gather.8.cloned.1.call-start = ((), (), s32[]{:S(2)}) async-start(), calls=%async_computation.6 | async-start | bytes 1966080 | tf_op jit(solution)/shard_map/all_gather | solution.py:79
  7.9 109.2 %all-gather.4.cloned.1.call-start = ((), (), s32[]{:S(2)}) async-start(), calls=%async_computation.4 | async-start | bytes 1966080 | tf_op jit(solution)/shard_map/all_gather | solution.py:77
  8.6 156.9 %all-gather.6.cloned.1.call-start = ((), (), s32[]{:S(2)}) async-start(), calls=%async_computation.5 | async-start | bytes 1966080 | tf_op jit(solution)/shard_map/all_gather | solution.py:78
  168.8 18.7 %all-to-all-start = ((bf16[32,1,56,128]{3,2,1,0:T(8,128)(2,1)}), bf16[32,1,56,128]{3,2,1,0:T(8,128)(2,1)S(1)}, u32[]{:S(2)}, u32[]{:S(2)}) async-start(bf16[32,1,56,128]{3,2,1,0:T(8,128)(2,1)} %bitcast.6), calls=%async_computation | async-start | bytes 917504 | tf_op jit(solution)/shard_map/all_to_all | solution.py:90
  187.5 14.6 %all-to-all-start.1 = ((bf16[32,1,56,128]{3,2,1,0:T(8,128)(2,1)}), bf16[32,1,56,128]{3,2,1,0:T(8,128)(2,1)S(1)}, u32[]{:S(2)}, u32[]{:S(2)}) async-start(bf16[32,1,56,128]{3,2,1,0:T(8,128)(2,1)} %bitcast.10), calls=%async_computation.1 | async-start | bytes 917504 | tf_op jit(solution)/shard_map/all_to_all | solution.py:91
  202.1 14.6 %all-to-all-start.2 = ((bf16[32,1,56,128]{3,2,1,0:T(8,128)(2,1)}), bf16[32,1,56,128]{3,2,1,0:T(8,128)(2,1)S(1)}, u32[]{:S(2)}, u32[]{:S(2)}) async-start(bf16[32,1,56,128]{3,2,1,0:T(8,128)(2,1)} %bitcast.13), calls=%async_computation.2 | async-start | bytes 917504 | tf_op jit(solution)/shard_map/all_to_all | solution.py:92
  233.6 26.3 %copy-start = (bf16[2,48,2048]{2,1,0:T(8,128)(2,1)S(1)}, bf16[2,48,2048]{2,1,0:T(8,128)(2,1)}, u32[]{:S(2)}) copy-start(bf16[2,48,2048]{2,1,0:T(8,128)(2,1)} %param.21) | copy-start | bytes 1179652
Sparse Core Ops, SparseCore 0:
  10.1 58.2 all-gather.7
  70.5 46.6 all-gather.3
  119.2 46.2 all-gather.5
where the time goes:
time: 268 us; the launch traced here: 267 us
  waiting for transfers between devices  141 us (53%)
  blocking collectives  55.1 us (21%)
  local copies, waits for them, and re-layouts  19.6 us (7%)
  starting transfers between devices  15.4 us (6%)
  other arithmetic  15.4 us (6%)
  between operations  14 us (5%)
  matrix products  6.71 us (3%)
    all_gather x1, waiting for transfers between devices, per_device(): lax.all_gather(video_query, 'dom', axis=0, tiled=True)  46.8 us
    all_gather x1, waiting for transfers between devices, per_device(): lax.all_gather(video_key, 'dom', axis=0, tiled=True)  46.4 us
    all_gather x1, waiting for transfers between devices, per_device(): lax.all_gather(video_value, 'dom', axis=0, tiled=True)  15.4 us
    all_gather x1, blocking collectives, per_device(): lax.all_gather(text_key, 'dom', axis=0, tiled=True)  15 us
    all_to_all x1, blocking collectives, token_layout(): lax.all_to_all(attended, 'seq', split_axis=2, concat_axis=0, tiled=True)  14.3 us
    all_gather x1, blocking collectives, per_device(): lax.all_gather(text_value, 'dom', axis=0, tiled=True)  13.8 us
    all_gather x1, blocking collectives, per_device(): lax.all_gather(text_query, 'dom', axis=0, tiled=True)  11.9 us
    all_to_all x1, waiting for transfers between devices, per_device(): lax.all_to_all(value_heads, 'seq', split_axis=0, concat_axis=2, tiled=True)  10.6 us
  transfers between devices with their start and end apart: 6, of which 6 were waited for; matrix products, arithmetic and copies ran while one was open for 3% of the time, Pallas kernels for 0%

commit v1 on v0

v1 whole, which is shorter than its diff:
```python
import functools

import jax
import jax.numpy as jnp
from jax import lax
from jax.experimental import pallas as pl
from jax.experimental.pallas import tpu as pltpu
from jax.sharding import PartitionSpec as P

HD = 128
LOG2E = 1.4426950408889634
VMEM_LIMIT = 48 * 2**20


def ancestors(counts):
    running = jnp.cumsum(counts)
    slot_ids = jnp.arange(counts.shape[0], dtype=jnp.int32)
    return jnp.sum((running[None, :] <= slot_ids[:, None]).astype(jnp.int32), axis=1)


def pack_kernel(vq, vk, vv, tq, tk, tv, out):
    rows, text = vq.shape[1], tq.shape[1]
    base = 3 * rows
    for p in range(vq.shape[0]):
        for h in range(vq.shape[2] // HD):
            columns = slice(h * HD, (h + 1) * HD)
            for i, ref in enumerate((vq, vk, vv)):
                out[p, h, i * rows : (i + 1) * rows, :] = ref[p, :, columns]
            for i, ref in enumerate((tq, tk, tv)):
                out[p, h, base + i * text : base + (i + 1) * text, :] = ref[p, :, columns]


def pack(vq, vk, vv, tq, tk, tv, steps=2):
    resident, rows, features = vq.shape
    text = tq.shape[1]
    heads = features // HD
    width = features // steps
    total = 3 * (rows + text)
    video = pl.BlockSpec((resident, rows, width), lambda i: (0, 0, i))
    words = pl.BlockSpec((resident, text, width), lambda i: (0, 0, i))
    packed = pl.pallas_call(
        pack_kernel,
        grid=(steps,),
        in_specs=[video] * 3 + [words] * 3,
        out_specs=pl.BlockSpec((resident, heads // steps, total, HD), lambda i: (0, i, 0, 0)),
        out_shape=jax.ShapeDtypeStruct((resident, heads, total, HD), vq.dtype),
        name="pack",
    )(vq, vk, vv, tq, tk, tv)
    return packed.reshape(resident * heads, total, HD)


def attend_kernel(x, out, q, k, v, *, rows, text, block):
    n = x.shape[0]
    video_rows, text_rows = n * rows, n * text
    total = video_rows + text_rows
    base = 3 * rows
    for i, ref in enumerate((q, k, v)):
        ref[0:video_rows, 0:HD] = x[:, i * rows : (i + 1) * rows, :].reshape(video_rows, HD)
        ref[video_rows:total, 0:HD] = x[:, base + i * text : base + (i + 1) * text, :].reshape(
            text_rows, HD
        )
    v[:, HD : 2 * HD] = jnp.ones((total, HD), v.dtype)
    scale = HD**-0.5 * LOG2E
    for start in range(0, total, block):
        piece = q[start : start + block, :]
        scores = lax.dot_general(
            piece, k[...], (((1,), (1,)), ((), ())), preferred_element_type=jnp.float32
        )
        row_max = jnp.max(scores, axis=1, keepdims=True)
        weights = jnp.exp2((scores - row_max) * scale).astype(v.dtype)
        summed = jnp.dot(weights, v[...], preferred_element_type=jnp.float32)
        q[start : start + block, :] = (summed[:, :HD] / summed[:, HD:]).astype(q.dtype)
    out[:, 0:rows, :] = q[0:video_rows, :].reshape(n, rows, HD)
    out[:, rows : rows + text, :] = q[video_rows:total, :].reshape(n, text, HD)


def attend(x, rows, text, block=256):
    n = x.shape[0]
    total = n * (rows + text)
    return pl.pallas_call(
        functools.partial(attend_kernel, rows=rows, text=text, block=block),
        in_specs=[pl.BlockSpec(memory_space=pltpu.VMEM)],
        out_specs=pl.BlockSpec(memory_space=pltpu.VMEM),
        out_shape=jax.ShapeDtypeStruct((n, rows + text, HD), x.dtype),
        scratch_shapes=[
            pltpu.VMEM((total, HD), x.dtype),
            pltpu.VMEM((total, HD), x.dtype),
            pltpu.VMEM((total, 2 * HD), x.dtype),
        ],
        compiler_params=pltpu.CompilerParams(vmem_limit_bytes=VMEM_LIMIT),
        name="attend",
    )(x)


def fetch(choice, slot, candidates, target, sem):
    start = 0
    for ref in candidates:
        for b in range(ref.shape[0]):

            @pl.when(choice[slot] == start + b)
            def _(ref=ref, b=b):
                pltpu.make_async_copy(ref.at[b], target, sem).start()

        start += ref.shape[0]


def select_kernel(choice, *refs):
    candidates, out, sems = refs[:-2], refs[-2], refs[-1]
    for s in range(out.shape[0]):
        fetch(choice, s, candidates, out.at[s], sems.at[s])
    for s in range(out.shape[0]):
        pltpu.make_async_copy(out.at[s], out.at[s], sems.at[s]).wait()


def select(choice, candidates):
    slots = choice.shape[0]
    return pl.pallas_call(
        select_kernel,
        grid_spec=pltpu.PrefetchScalarGridSpec(
            num_scalar_prefetch=1,
            grid=(1,),
            in_specs=[pl.BlockSpec(memory_space=pl.ANY)] * len(candidates),
            out_specs=pl.BlockSpec(memory_space=pl.ANY),
            scratch_shapes=[pltpu.SemaphoreType.DMA((slots,))],
        ),
        out_shape=jax.ShapeDtypeStruct((slots,) + candidates[0].shape[1:], candidates[0].dtype),
        name="select",
    )(choice, *candidates)


def finish_kernel(choice, *refs):
    candidates, (noise, video, words, held, sems) = refs[:-5], refs[-5:]
    slots, rows = noise.shape[0], noise.shape[1]
    text = words.shape[1]
    for s in range(slots):
        fetch(choice, s, candidates, held.at[s], sems.at[s])
    for s in range(slots):
        pltpu.make_async_copy(held.at[s], held.at[s], sems.at[s]).wait()
        for h in range(held.shape[1]):
            columns = slice(h * HD, (h + 1) * HD)
            total = held[s, h, 0:rows, :].astype(jnp.float32) + noise[s, :, columns].astype(
                jnp.float32
            )
            video[s, :, columns] = total.astype(video.dtype)
            words[s, :, columns] = held[s, h, rows : rows + text, :]


def finish(choice, candidates, noise, text):
    slots, rows, features = noise.shape
    whole = lambda *shape: pl.BlockSpec(shape, lambda i, c: (0, 0, 0))
    return pl.pallas_call(
        finish_kernel,
        grid_spec=pltpu.PrefetchScalarGridSpec(
            num_scalar_prefetch=1,
            grid=(1,),
            in_specs=[pl.BlockSpec(memory_space=pl.ANY)] * len(candidates)
            + [whole(slots, rows, features)],
            out_specs=[whole(slots, rows, features), whole(slots, text, features)],
            scratch_shapes=[
                pltpu.VMEM((slots,) + candidates[0].shape[1:], candidates[0].dtype),
                pltpu.SemaphoreType.DMA((slots,)),
            ],
        ),
        out_shape=[
            jax.ShapeDtypeStruct(noise.shape, noise.dtype),
            jax.ShapeDtypeStruct((slots, text, features), noise.dtype),
        ],
        name="finish",
    )(choice, *candidates, noise)


def per_device(
    counts, video_query, video_key, video_value, text_query, text_key, text_value, fresh_noise
):
    resident, rows, features = video_query.shape
    text = text_query.shape[1]
    heads = features // HD
    lineage = ancestors(counts)
    dom = lax.axis_index("dom")

    packed = pack(video_query, video_key, video_value, text_query, text_key, text_value)
    gathered = lax.all_to_all(packed, "seq", split_axis=0, concat_axis=0, tiled=True)
    attended = attend(gathered, rows, text)
    returned = lax.all_to_all(attended, "seq", split_axis=0, concat_axis=0, tiled=True)
    own = returned.reshape(resident, heads, rows + text, HD)

    near = lax.ppermute(own, "dom", [(0, 1), (1, 2)])
    second = lax.ppermute(own[1:], "dom", [(0, 2)])
    mine = lax.dynamic_slice_in_dim(lineage, dom * resident, resident)
    tail = lineage[6:8]
    onward = jnp.where(tail == 1, 4, jnp.where(tail < 4, tail, jnp.where(tail < 6, tail - 4, 0)))
    onward = jnp.where(dom == 2, onward, jnp.arange(resident, dtype=jnp.int32))
    last = lax.ppermute(select(onward, (own, near, second)), "dom", [(2, 3), (3, 2)])
    place = jnp.arange(resident, dtype=jnp.int32)
    choice = jnp.where(
        dom == 0,
        mine,
        jnp.where(
            dom == 1,
            mine + 2,
            jnp.where(
                dom == 2,
                jnp.where(
                    mine == 1, 4, jnp.where(mine < 4, mine, jnp.where(mine < 6, mine - 4, mine - 1))
                ),
                jnp.where(mine < 6, 5 + place, mine - 6),
            ),
        ),
    )
    video_out, text_out = finish(choice, (own, near, second, last), fresh_noise, text)
    return video_out, text_out


def solution(mesh):
    placed = P(("rep", "dom"), "seq", None)
    return jax.shard_map(
        per_device,
        mesh=mesh,
        in_specs=(P("rep"),) + (placed,) * 7,
        out_specs=(placed, placed),
        check_vma=False,
    )
```

time: 268 us -> 107 us (0.40)
  the two profiles are of different devices: /device:TPU:1 before, /device:TPU:320 now
where the time goes in v1:
time: 107 us; the launch traced here: 106 us
  waiting for transfers between devices  39.8 us (37%)
  blocking collectives  28 us (26%)
  Pallas kernels  27 us (25%)
  starting transfers between devices  8.38 us (8%)
  local copies, waits for them, and re-layouts  1.63 us (2%)
    all_to_all x1, blocking collectives, per_device(): lax.all_to_all(packed, 'seq', split_axis=0, concat_axis=0, tiled=True)  28 us
    ppermute x1, waiting for transfers between devices, per_device(): second = lax.ppermute(own[1:], 'dom', [(0, 2)])  17 us
    pallas_call x1, Pallas kernels, select(): pl.pallas_call(select_kernel, grid_spec=pltpu.PrefetchScalarGridSpec(num_...  15.7 us
    ppermute x1, waiting for transfers between devices, per_device(): lax.ppermute(select(onward, (own, near, second)), 'dom', [(2, 3), (3, 2)])  12.4 us
    all_to_all x1, waiting for transfers between devices, per_device(): lax.all_to_all(attended, 'seq', split_axis=0, concat_axis=0, tiled=True)  10.4 us
    pallas_call x1, Pallas kernels, attend(): pl.pallas_call(functools.partial(attend_kernel, rows=rows, text=text, blo...  5.35 us
    all_to_all x1, starting transfers between devices, per_device(): lax.all_to_all(attended, 'seq', split_axis=0, concat_axis=0, tiled=True)  3.88 us
    pallas_call x1, Pallas kernels, finish(): pl.pallas_call(finish_kernel, grid_spec=pltpu.PrefetchScalarGridSpec(num_...  3.52 us
  transfers between devices with their start and end apart: 4, of which 3 were waited for; matrix products, arithmetic and copies ran while one was open for 1% of the time, Pallas kernels for 0%

profile of v1, /device:TPU:320, one launch (start us, length us, event | category | flops | bytes accessed | tf_op | source)
XLA Modules:
  0.0 106.4 jit_solution(2501758431773879868)
XLA Ops:
  0.6 2.4 %pack.1 = bf16[2,16,168,128]{3,2,1,0:T(8,128)(2,1)} custom-call(bf16[2,48,2048]{2,1,0:T(8,128)(2,1)} %vq.1, bf16[2,48,2048]{2,1,0:T(8,128)(2,1)} %vk.1, bf16[2,48,2048]{2,1,0:T(8,128)(2,1)} %vv.1, bf16[2,8,2048]{2,1,0:T(8,128)(2,1)} %tq.1, bf16[2,8,2048]{2,1,0:T(8,128)(2,1)} %tk.1, bf16[2,8,2048]{2,1,0:T(8,128)(2,1)} %tv.1), custom_call_target="tpu_custom_call" | custom-call | tf_op jit(solution)/shard_map/pack/pallas_call | solution.py:41
  3.1 28.0 %all_to_all.10.x = bf16[32,168,128]{2,1,0:T(8,128)(2,1)S(1)} all-to-all(bf16[32,168,128]{2,1,0:T(8,128)(2,1)} %bitcast.9), channel_id=1, replica_groups=mesh['dom'=4,'seq'=32,'rep'=4] {'seq'}, dimensions={0} | all-to-all | bytes 2752512 | tf_op jit(solution)/shard_map/all_to_all | solution.py:182
  31.0 0.0 copy-start.4
  31.0 5.3 %attend.1 = bf16[32,56,128]{2,1,0:T(8,128)(2,1)} custom-call(bf16[32,168,128]{2,1,0:T(8,128)(2,1)S(1)} %all_to_all.10.x), custom_call_target="tpu_custom_call" | custom-call | tf_op jit(solution)/shard_map/attend/pallas_call | solution.py:80
  36.4 3.9 %all-to-all-start.1 = ((bf16[32,56,128]{2,1,0:T(8,128)(2,1)}), bf16[32,56,128]{2,1,0:T(8,128)(2,1)S(1)}, u32[]{:S(2)}, u32[]{:S(2)}) async-start(bf16[32,56,128]{2,1,0:T(8,128)(2,1)} %attend.1), calls=%async_computation.1 | async-start | bytes 917504 | tf_op jit(solution)/shard_map/all_to_all | solution.py:184
  40.3 0.0 copy-done.4
  40.3 0.2 reduce-window.8
  40.5 10.4 %all-to-all-done.1 = bf16[32,56,128]{2,1,0:T(8,128)(2,1)S(1)} async-done(((bf16[32,56,128]{2,1,0:T(8,128)(2,1)}), bf16[32,56,128]{2,1,0:T(8,128)(2,1)S(1)}, u32[]{:S(2)}, u32[]{:S(2)}) %all-to-all-start.1) | async-done | bytes 458784 | tf_op jit(solution)/shard_map/all_to_all | solution.py:184
  50.8 0.0 copy-start
  50.8 1.3 %collective-permute-start = (bf16[2,16,56,128]{3,2,1,0:T(8,128)(2,1)S(1)}, bf16[2,16,56,128]{3,2,1,0:T(8,128)(2,1)S(1)}, u32[]{:S(2)}, u32[]{:S(2)}) collective-permute-start(bf16[2,16,56,128]{3,2,1,0:T(8,128)(2,1)S(1)} %bitcast.6), channel_id=1, source_target_pairs={{0,128},{128,256},{1,129},{129,257},{2,130},{130,258},{3,131},{131... | collective-permute-start | bytes 1376264 | tf_op jit(solution)/shard_map/ppermute | solution.py:187
  52.1 1.3 %collective-permute-start.1 = (bf16[1,16,56,128]{3,2,1,0:T(8,128)(2,1)S(1)}, bf16[1,16,56,128]{3,2,1,0:T(8,128)(2,1)S(1)}, u32[]{:S(2)}, u32[]{:S(2)}) collective-permute-start(bf16[1,16,56,128]{3,2,1,0:T(8,128)(2,1)S(1)} %slice_bitcast_fusion), channel_id=1, source_target_pairs={{0,256},{1,257},{2,258},{3,259},{4,260},{5,261},{6,262},{7,263},{8... | collective-permute-start | bytes 688136 | tf_op jit(solution)/shard_map/ppermute | solution.py:188
  53.4 0.1 convert_reduce_fusion
  53.6 0.6 broadcast_select_fusion
  54.2 17.0 %collective-permute-done.1.refs_2_ = bf16[1,16,56,128]{3,2,1,0:T(8,128)(2,1)S(1)} collective-permute-done((bf16[1,16,56,128]{3,2,1,0:T(8,128)(2,1)S(1)}, bf16[1,16,56,128]{3,2,1,0:T(8,128)(2,1)S(1)}, u32[]{:S(2)}, u32[]{:S(2)}) %collective-permute-start.1) | collective-permute-done | bytes 229408 | tf_op jit(solution)/shard_map/ppermute | solution.py:188
  71.2 0.0 copy-start.2
  71.2 0.0 collective-permute-done.refs_1_
  71.2 0.0 copy-done
  71.2 0.7 copy-done.2
  71.9 0.2 copy-done.1
  72.0 15.7 %select.1 = bf16[2,16,56,128]{3,2,1,0:T(8,128)(2,1)} custom-call(s32[2]{0:T(128)} %get-tuple-element.2.choice, bf16[2,16,56,128]{3,2,1,0:T(8,128)(2,1)} %bitcast.7, bf16[2,16,56,128]{3,2,1,0:T(8,128)(2,1)} %copy-done.1, bf16[1,16,56,128]{3,2,1,0:T(8,128)(2,1)} %copy-done.2), custom_call_target="tpu_custom_call" | custom-call | tf_op jit(solution)/shard_map/select/pallas_call | solution.py:117
  87.7 1.9 %collective-permute-start.2 = (bf16[2,16,56,128]{3,2,1,0:T(8,128)(2,1)}, bf16[2,16,56,128]{3,2,1,0:T(8,128)(2,1)S(1)}, u32[]{:S(2)}, u32[]{:S(2)}) collective-permute-start(bf16[2,16,56,128]{3,2,1,0:T(8,128)(2,1)} %select.1), channel_id=1, source_target_pairs={{256,384},{384,256},{257,385},{385,257},{258,386},{386,258},{259,3... | collective-permute-start | bytes 1376264 | tf_op jit(solution)/shard_map/ppermute | solution.py:193
  89.6 12.4 %collective-permute-done.2.refs_3_ = bf16[2,16,56,128]{3,2,1,0:T(8,128)(2,1)S(1)} collective-permute-done((bf16[2,16,56,128]{3,2,1,0:T(8,128)(2,1)}, bf16[2,16,56,128]{3,2,1,0:T(8,128)(2,1)S(1)}, u32[]{:S(2)}, u32[]{:S(2)}) %collective-permute-start.2) | collective-permute-done | bytes 458784 | tf_op jit(solution)/shard_map/ppermute | solution.py:193
  102.1 0.8 copy-done.3
  102.9 3.5 %finish.1 = (bf16[2,48,2048]{2,1,0:T(8,128)(2,1)}, bf16[2,8,2048]{2,1,0:T(8,128)(2,1)}) custom-call(s32[2]{0:T(128)} %get-tuple-element.3.choice, bf16[2,16,56,128]{3,2,1,0:T(8,128)(2,1)} %bitcast.8, bf16[2,16,56,128]{3,2,1,0:T(8,128)(2,1)} %copy-done.1, bf16[1,16,56,128]{3,2,1,0:T(8,128)(2,1)} %copy-done.2, bf16[2,16,56,128]{3,2,1,0:T(8,128)(2,1)} %copy-done.3, ...), custom_call_target="tpu_custom_call" | custom-call | tf_op jit(solution)/shard_map/finish/pallas_call | solution.py:151
  (3 shorter events, 0.0 us)
Async XLA Ops:
  31.0 9.2 %copy-start.4 = (s32[8]{0:T(128)S(1)}, s32[8]{0:T(128)}, u32[]{:S(2)}) copy-start(s32[8]{0:T(128)} %param.8) | copy-start | bytes 100
  36.4 14.4 %all-to-all-start.1 = ((bf16[32,56,128]{2,1,0:T(8,128)(2,1)}), bf16[32,56,128]{2,1,0:T(8,128)(2,1)S(1)}, u32[]{:S(2)}, u32[]{:S(2)}) async-start(bf16[32,56,128]{2,1,0:T(8,128)(2,1)} %attend.1), calls=%async_computation.1 | async-start | bytes 917504 | tf_op jit(solution)/shard_map/all_to_all | solution.py:184
  50.8 20.4 %copy-start = (bf16[32,56,128]{2,1,0:T(8,128)(2,1)}, bf16[32,56,128]{2,1,0:T(8,128)(2,1)S(1)}, u32[]{:S(2)}) copy-start(bf16[32,56,128]{2,1,0:T(8,128)(2,1)S(1)} %all-to-all-done.1) | copy-start | bytes 1376260
  50.8 20.4 %collective-permute-start = (bf16[2,16,56,128]{3,2,1,0:T(8,128)(2,1)S(1)}, bf16[2,16,56,128]{3,2,1,0:T(8,128)(2,1)S(1)}, u32[]{:S(2)}, u32[]{:S(2)}) collective-permute-start(bf16[2,16,56,128]{3,2,1,0:T(8,128)(2,1)S(1)} %bitcast.6), channel_id=1, source_target_pairs={{0,128},{128,256},{1,129},{129,257},{2,130},{130,258},{3,131},{131... | collective-permute-start | bytes 1376264 | tf_op jit(solution)/shard_map/ppermute | solution.py:187
  52.1 19.0 %collective-permute-start.1 = (bf16[1,16,56,128]{3,2,1,0:T(8,128)(2,1)S(1)}, bf16[1,16,56,128]{3,2,1,0:T(8,128)(2,1)S(1)}, u32[]{:S(2)}, u32[]{:S(2)}) collective-permute-start(bf16[1,16,56,128]{3,2,1,0:T(8,128)(2,1)S(1)} %slice_bitcast_fusion), channel_id=1, source_target_pairs={{0,256},{1,257},{2,258},{3,259},{4,260},{5,261},{6,262},{7,263},{8... | collective-permute-start | bytes 688136 | tf_op jit(solution)/shard_map/ppermute | solution.py:188
  71.2 0.7 copy-start.2
  71.2 0.8 copy-start.1
  87.7 14.4 %collective-permute-start.2 = (bf16[2,16,56,128]{3,2,1,0:T(8,128)(2,1)}, bf16[2,16,56,128]{3,2,1,0:T(8,128)(2,1)S(1)}, u32[]{:S(2)}, u32[]{:S(2)}) collective-permute-start(bf16[2,16,56,128]{3,2,1,0:T(8,128)(2,1)} %select.1), channel_id=1, source_target_pairs={{256,384},{384,256},{257,385},{385,257},{258,386},{386,258},{259,3... | collective-permute-start | bytes 1376264 | tf_op jit(solution)/shard_map/ppermute | solution.py:193
  102.1 0.8 copy-start.3

commit v2 on v1

v2 whole, which is shorter than its diff:
```python
import functools
import itertools

import jax
import jax.numpy as jnp
from jax import lax
from jax.experimental import pallas as pl
from jax.experimental.pallas import tpu as pltpu
from jax.sharding import PartitionSpec as P

HD = 128
LOG2E = 1.4426950408889634
VMEM_LIMIT = 48 * 2**20


def lineages(slots):
    half = slots // 2
    rows = set()
    for other in range(1, half + 1):
        for first, second in ((half, other), (other, half)):
            rest = slots - first - second
            for tail in itertools.combinations_with_replacement(range(2, slots), rest):
                rows.add((0,) * first + (1,) * second + tail)
    return sorted(rows)


def transfers(row):
    pairs = []
    for plane in range(1, len(row) // 2):
        wanted = sorted(set(row[2 * plane : 2 * plane + 2]))
        pairs += [(p // 2, plane) for p in wanted if p // 2 != plane]
    return tuple(sorted(pairs))


def key_of(row):
    as_int = lambda flag: jnp.where(flag, 1, 0) if isinstance(flag, jax.Array) else int(flag)
    key = as_int(row[2] != row[3])
    key = key + 2 * as_int(row[5] // 2 == 1) + 4 * as_int(row[5] // 2 == 3)
    key = key + 8 * as_int(row[6] // 2 == 0)
    for plane, weight in ((1, 16), (2, 48)):
        from_six = as_int(row[6] // 2 == plane)
        from_seven = as_int(row[7] // 2 == plane)
        same = as_int(row[6] == row[7])
        key = key + weight * (from_six + from_seven - from_six * same)
    return key


def plans(slots):
    found = {}
    for row in lineages(slots):
        found[key_of(row)] = transfers(row)
    out = []
    for key in sorted(found):
        rounds = []
        seen = {}
        for pair in sorted(found[key], key=lambda p: -abs(p[1] - p[0])):
            which = seen.get(pair, 0)
            seen[pair] = which + 1
            for members in rounds:
                if all(pair[0] != m[0] and pair[1] != m[1] for m in members):
                    members.append(pair + (which,))
                    break
            else:
                rounds.append([pair + (which,)])
        out.append((key, rounds))
    return out


def pack_kernel(counts, vq, vk, vv, tq, tk, tv, out, facts, *, keys):
    @pl.when(pl.program_id(0) == 0)
    def _():
        slots = counts.shape[0]
        running = [counts[0]]
        for i in range(1, slots):
            running.append(running[-1] + counts[i])
        row = [sum(jnp.where(r <= j, 1, 0) for r in running) for j in range(slots)]
        facts[0] = lax.axis_index("dom")
        for j in range(slots):
            facts[1 + j] = row[j]
        key = key_of(row)
        facts[1 + slots] = sum(jnp.where(key == k, i, 0) for i, k in enumerate(keys))

    rows, text = vq.shape[1], tq.shape[1]
    base = 3 * rows
    for p in range(vq.shape[0]):
        for h in range(vq.shape[2] // HD):
            columns = slice(h * HD, (h + 1) * HD)
            for i, ref in enumerate((vq, vk, vv)):
                out[p, h, i * rows : (i + 1) * rows, :] = ref[p, :, columns]
            for i, ref in enumerate((tq, tk, tv)):
                out[p, h, base + i * text : base + (i + 1) * text, :] = ref[p, :, columns]


def pack(counts, vq, vk, vv, tq, tk, tv, keys, steps=2):
    resident, rows, features = vq.shape
    text = tq.shape[1]
    heads = features // HD
    width = features // steps
    total = 3 * (rows + text)
    video = pl.BlockSpec((resident, rows, width), lambda i: (0, 0, i))
    words = pl.BlockSpec((resident, text, width), lambda i: (0, 0, i))
    scalars = pl.BlockSpec(memory_space=pltpu.SMEM)
    packed, facts = pl.pallas_call(
        functools.partial(pack_kernel, keys=keys),
        grid=(steps,),
        in_specs=[scalars] + [video] * 3 + [words] * 3,
        out_specs=[
            pl.BlockSpec((resident, heads // steps, total, HD), lambda i: (0, i, 0, 0)),
            scalars,
        ],
        out_shape=[
            jax.ShapeDtypeStruct((resident, heads, total, HD), vq.dtype),
            jax.ShapeDtypeStruct((counts.shape[0] + 2,), jnp.int32),
        ],
        name="pack",
    )(counts, vq, vk, vv, tq, tk, tv)
    return packed.reshape(resident * heads, total, HD), facts


def attend_kernel(x, out, q, k, v, *, rows, text, block):
    n = x.shape[0]
    video_rows, text_rows = n * rows, n * text
    total = video_rows + text_rows
    base = 3 * rows
    for i, ref in enumerate((q, k, v)):
        ref[0:video_rows, 0:HD] = x[:, i * rows : (i + 1) * rows, :].reshape(video_rows, HD)
        ref[video_rows:total, 0:HD] = x[:, base + i * text : base + (i + 1) * text, :].reshape(
            text_rows, HD
        )
    v[:, HD : 2 * HD] = jnp.ones((total, HD), v.dtype)
    scale = HD**-0.5 * LOG2E
    for start in range(0, total, block):
        piece = q[start : start + block, :]
        scores = lax.dot_general(
            piece, k[...], (((1,), (1,)), ((), ())), preferred_element_type=jnp.float32
        )
        row_max = jnp.max(scores, axis=1, keepdims=True)
        weights = jnp.exp2((scores - row_max) * scale).astype(v.dtype)
        summed = jnp.dot(weights, v[...], preferred_element_type=jnp.float32)
        q[start : start + block, :] = (summed[:, :HD] / summed[:, HD:]).astype(q.dtype)
    out[:, 0:rows, :] = q[0:video_rows, :].reshape(n, rows, HD)
    out[:, rows : rows + text, :] = q[video_rows:total, :].reshape(n, text, HD)


def attend(x, rows, text, block=256):
    n = x.shape[0]
    total = n * (rows + text)
    return pl.pallas_call(
        functools.partial(attend_kernel, rows=rows, text=text, block=block),
        in_specs=[pl.BlockSpec(memory_space=pltpu.VMEM)],
        out_specs=pl.BlockSpec(memory_space=pltpu.VMEM),
        out_shape=jax.ShapeDtypeStruct((n, rows + text, HD), x.dtype),
        scratch_shapes=[
            pltpu.VMEM((total, HD), x.dtype),
            pltpu.VMEM((total, HD), x.dtype),
            pltpu.VMEM((total, 2 * HD), x.dtype),
        ],
        compiler_params=pltpu.CompilerParams(vmem_limit_bytes=VMEM_LIMIT),
        name="attend",
    )(x)


def outgoing_kernel(facts, own, *sends, rounds):
    dom = facts[0]
    for members, send in zip(rounds, sends):
        index = 0
        for source, target, which in members:
            slot = 1 + 2 * target
            if which == 0:
                wanted = jnp.where(facts[slot] // 2 == source, facts[slot], facts[slot + 1])
            else:
                wanted = facts[slot + 1]
            index = jnp.where(dom == source, lax.rem(wanted, 2), index)
        send[...] = own[index]


def outgoing(facts, own, rounds):
    vmem = pl.BlockSpec(memory_space=pltpu.VMEM)
    block = jax.ShapeDtypeStruct(own.shape[1:], own.dtype)
    return pl.pallas_call(
        functools.partial(outgoing_kernel, rounds=rounds),
        in_specs=[pl.BlockSpec(memory_space=pltpu.SMEM), vmem],
        out_specs=[vmem] * len(rounds),
        out_shape=[block] * len(rounds),
        name="outgoing",
    )(facts, own)


def finish_kernel(facts, own, *refs, rounds):
    received, (noise, video, words) = refs[:-3], refs[-3:]
    slots, rows = noise.shape[0], noise.shape[1]
    text = words.shape[1]
    dom = facts[0]
    for s in range(slots):
        ancestor = facts[1 + 2 * dom + s]
        origin = ancestor // 2
        chosen = 0
        for r, members in enumerate(rounds):
            for source, target, which in members:
                twice = sum(m[:2] == (source, target) for ms in rounds for m in ms) == 2
                if not twice or which == s:
                    hit = jnp.logical_and(dom == target, origin == source)
                    chosen = jnp.where(hit, 1 + r, chosen)

        def write(block, s=s):
            for h in range(own.shape[1]):
                columns = slice(h * HD, (h + 1) * HD)
                part = block[h, 0:rows, :].astype(jnp.float32)
                total = part + noise[s, :, columns].astype(jnp.float32)
                video[s, :, columns] = total.astype(video.dtype)
                words[s, :, columns] = block[h, rows : rows + text, :]

        @pl.when(chosen == 0)
        def _(write=write, ancestor=ancestor):
            write(own.at[lax.rem(ancestor, 2)])

        for r, block in enumerate(received):

            @pl.when(chosen == 1 + r)
            def _(write=write, block=block):
                write(block)


def finish(facts, own, received, noise, text, rounds):
    slots, _, features = noise.shape
    vmem = pl.BlockSpec(memory_space=pltpu.VMEM)
    return pl.pallas_call(
        functools.partial(finish_kernel, rounds=rounds),
        in_specs=[pl.BlockSpec(memory_space=pltpu.SMEM)] + [vmem] * (2 + len(received)),
        out_specs=[vmem, vmem],
        out_shape=[
            jax.ShapeDtypeStruct(noise.shape, noise.dtype),
            jax.ShapeDtypeStruct((slots, text, features), noise.dtype),
        ],
        name="finish",
    )(facts, own, *received, noise)


def resample(rounds, text, facts, own, noise):
    sends = outgoing(facts, own, rounds)
    received = [
        lax.ppermute(send, "dom", [m[:2] for m in members]) for send, members in zip(sends, rounds)
    ]
    return tuple(finish(facts, own, received, noise, text, rounds))


def per_device(
    counts, video_query, video_key, video_value, text_query, text_key, text_value, fresh_noise
):
    resident, rows, features = video_query.shape
    text = text_query.shape[1]
    heads = features // HD
    known = plans(counts.shape[0])

    packed, facts = pack(
        counts,
        video_query,
        video_key,
        video_value,
        text_query,
        text_key,
        text_value,
        [key for key, _ in known],
    )
    gathered = lax.all_to_all(packed, "seq", split_axis=0, concat_axis=0, tiled=True)
    attended = attend(gathered, rows, text)
    returned = lax.all_to_all(attended, "seq", split_axis=0, concat_axis=0, tiled=True)
    own = returned.reshape(resident, heads, rows + text, HD)
    branches = [functools.partial(resample, rounds, text) for _, rounds in known]
    return lax.switch(facts[counts.shape[0] + 1], branches, facts, own, fresh_noise)


def solution(mesh):
    placed = P(("rep", "dom"), "seq", None)
    return jax.shard_map(
        per_device,
        mesh=mesh,
        in_specs=(P("rep"),) + (placed,) * 7,
        out_specs=(placed, placed),
        check_vma=False,
    )
```

time: 107 us -> 82.1 us (0.77)
  the two profiles are of different devices: /device:TPU:320 before, /device:TPU:352 now
where the time goes in v2:
time: 82.1 us; the launch traced here: 81.8 us
  waiting for transfers between devices  32.3 us (39%)
  blocking collectives  28 us (34%)
  Pallas kernels  11.6 us (14%)
  starting transfers between devices  7.19 us (9%)
  between operations  1.3 us (2%)
  local copies, waits for them, and re-layouts  1.29 us (2%)
    all_to_all x1, blocking collectives, per_device(): lax.all_to_all(packed, 'seq', split_axis=0, concat_axis=0, tiled=True)  28 us
    ppermute x4, waiting for transfers between devices, resample(): lax.ppermute(send, 'dom', [m[:2] for m in members])  23 us
    all_to_all x1, waiting for transfers between devices, per_device(): lax.all_to_all(attended, 'seq', split_axis=0, concat_axis=0, tiled=True)  9.31 us
    pallas_call x1, Pallas kernels, attend(): pl.pallas_call(functools.partial(attend_kernel, rows=rows, text=text, blo...  5.38 us
    all_to_all x1, starting transfers between devices, per_device(): lax.all_to_all(attended, 'seq', split_axis=0, concat_axis=0, tiled=True)  3.89 us
    ppermute x4, starting transfers between devices, resample(): lax.ppermute(send, 'dom', [m[:2] for m in members])  3.31 us
    pallas_call x1, Pallas kernels, pack(): pl.pallas_call(functools.partial(pack_kernel, keys=keys), grid=(steps,),...  2.48 us
    pallas_call x1, Pallas kernels, finish(): pl.pallas_call(functools.partial(finish_kernel, rounds=rounds), in_specs=...  2.22 us
  transfers between devices with their start and end apart: 5, of which 2 were waited for; matrix products, arithmetic and copies ran while one was open for 1% of the time, Pallas kernels for 0%

profile of v2, /device:TPU:352, one launch (start us, length us, event | category | flops | bytes accessed | tf_op | source)
XLA Modules:
  0.0 81.8 jit_solution(2580137480735369645)
XLA Ops:
  0.6 2.5 %pack.1 = (bf16[2,16,168,128]{3,2,1,0:T(8,128)(2,1)}, s32[10]{0:T(128)S(1)}) custom-call(s32[8]{0:T(128)} %counts.1, bf16[2,48,2048]{2,1,0:T(8,128)(2,1)} %vq.1, bf16[2,48,2048]{2,1,0:T(8,128)(2,1)} %vk.1, bf16[2,48,2048]{2,1,0:T(8,128)(2,1)} %vv.1, bf16[2,8,2048]{2,1,0:T(8,128)(2,1)} %tq.1, bf16[2,8,2048]{2,1,0:T(8,128)(2,1)} %tk.1, bf16[2,8,2048]{2,1,0:T(8,128)(2,1)} %tv.1), custom_call_target="tpu_custom_call" | custom-call | tf_op jit(solution)/shard_map/pack/pallas_call | solution.py:103
  3.1 28.0 %all_to_all.10.x = bf16[32,168,128]{2,1,0:T(8,128)(2,1)S(1)} all-to-all(bf16[32,168,128]{2,1,0:T(8,128)(2,1)} %bitcast.59), channel_id=1, replica_groups=mesh['dom'=4,'seq'=32,'rep'=4] {'seq'}, dimensions={0} | all-to-all | bytes 2752512 | tf_op jit(solution)/shard_map/all_to_all | solution.py:265
  31.1 5.4 %attend.1 = bf16[32,56,128]{2,1,0:T(8,128)(2,1)} custom-call(bf16[32,168,128]{2,1,0:T(8,128)(2,1)S(1)} %all_to_all.10.x), custom_call_target="tpu_custom_call" | custom-call | tf_op jit(solution)/shard_map/attend/pallas_call | solution.py:148
  36.5 3.9 %all-to-all-start.1 = ((bf16[32,56,128]{2,1,0:T(8,128)(2,1)}), bf16[32,56,128]{2,1,0:T(8,128)(2,1)S(1)}, u32[]{:S(2)}, u32[]{:S(2)}) async-start(bf16[32,56,128]{2,1,0:T(8,128)(2,1)} %attend.1), calls=%async_computation.1 | async-start | bytes 917504 | tf_op jit(solution)/shard_map/all_to_all | solution.py:267
  40.4 0.6 slice.3
  41.6 9.3 %all-to-all-done.1 = bf16[32,56,128]{2,1,0:T(8,128)(2,1)S(1)} async-done(((bf16[32,56,128]{2,1,0:T(8,128)(2,1)}), bf16[32,56,128]{2,1,0:T(8,128)(2,1)S(1)}, u32[]{:S(2)}, u32[]{:S(2)}) %all-to-all-start.1) | async-done | bytes 458784 | tf_op jit(solution)/shard_map/all_to_all | solution.py:267
  50.9 0.0 copy-done
  50.9 30.8 %conditional.1 = ((bf16[2,48,2048]{2,1,0:T(8,128)(2,1)}, bf16[2,8,2048]{2,1,0:T(8,128)(2,1)})) conditional(s32[]{:T(128)} %bitcast.19, (s32[10]{0:T(128)S(1)}, bf16[32,56,128]{2,1,0:T(8,128)(2,1)S(1)}, bf16[2,48,2048]{2,1,0:T(8,128)(2,1)S(1)}) %tuple.141, (s32[10]{0:T(128)S(1)}, bf16[32,56,128]{2,1,0:T(8,128)(2,1)S(1)}, ...), branch_computations={%region_0.0_spmd, %region_1.0_spmd, %region_2.0_spmd, %region_3.0_... | conditional | bytes 7340312 | solution.py:270
  50.9 1.5 %outgoing.23 = (bf16[16,56,128]{2,1,0:T(8,128)(2,1)}, bf16[16,56,128]{2,1,0:T(8,128)(2,1)}, bf16[16,56,128]{2,1,0:T(8,128)(2,1)}, bf16[16,56,128]{2,1,0:T(8,128)(2,1)}) custom-call(s32[10]{0:T(128)S(1)} %get-tuple-element.135.facts, bf16[2,16,56,128]{3,2,1,0:T(8,128)(2,1)S(1)} %bitcast.29), custom_call_target="tpu_custom_call" | custom-call | tf_op jit(solution)/shard_map/cond/branch_4_fun/outgoing/pallas_call | solution.py:180
  52.5 0.7 collective-permute-start.10
  53.1 0.7 collective-permute-start.11
  53.8 0.7 collective-permute-start.12
  54.5 1.3 %collective-permute-start.9 = (bf16[16,56,128]{2,1,0:T(8,128)(2,1)}, bf16[16,56,128]{2,1,0:T(8,128)(2,1)S(1)}, u32[]{:S(2)}, u32[]{:S(2)}) collective-permute-start(bf16[16,56,128]{2,1,0:T(8,128)(2,1)} %get-tuple-element.137), channel_id=1, source_target_pairs={{0,384},{1,385},{2,386},{3,387},{4,388},{5,389},{6,390},{7,391},{8... | collective-permute-start | bytes 688136 | tf_op jit(solution)/shard_map/cond/branch_4_fun/ppermute | solution.py:242
  55.8 0.0 collective-permute-done.10.refs_1_
  55.8 0.0 copy-start.25
  55.8 0.0 collective-permute-done.11.refs_2_
  55.8 0.0 copy-start.28
  55.8 0.0 collective-permute-done.12.refs_3_
  55.8 0.0 copy-start.31
  55.9 23.0 %collective-permute-done.9.refs_0_ = bf16[16,56,128]{2,1,0:T(8,128)(2,1)S(1)} collective-permute-done((bf16[16,56,128]{2,1,0:T(8,128)(2,1)}, bf16[16,56,128]{2,1,0:T(8,128)(2,1)S(1)}, u32[]{:S(2)}, u32[]{:S(2)}) %collective-permute-start.9) | collective-permute-done | bytes 229408 | tf_op jit(solution)/shard_map/cond/branch_4_fun/ppermute | solution.py:242
  78.8 0.0 copy-done.25
  78.8 0.0 copy-done.28
  78.8 0.7 copy-done.38
  79.5 2.2 %finish.23 = (bf16[2,48,2048]{2,1,0:T(8,128)(2,1)}, bf16[2,8,2048]{2,1,0:T(8,128)(2,1)}) custom-call(s32[10]{0:T(128)S(1)} %get-tuple-element.135.facts, bf16[2,16,56,128]{3,2,1,0:T(8,128)(2,1)S(1)} %bitcast.30, bf16[16,56,128]{2,1,0:T(8,128)(2,1)} %copy-done.38, bf16[16,56,128]{2,1,0:T(8,128)(2,1)} %copy-done.25, bf16[16,56,128]{2,1,0:T(8,128)(2,1)} %copy-done.28, ...), custom_call_target="tpu_custom_call" | custom-call | tf_op jit(solution)/shard_map/cond/branch_4_fun/finish/pallas_call | solution.py:227
  (3 shorter events, 0.0 us)
Async XLA Ops:
  31.1 19.8 %copy-start = (bf16[2,48,2048]{2,1,0:T(8,128)(2,1)S(1)}, bf16[2,48,2048]{2,1,0:T(8,128)(2,1)}, u32[]{:S(2)}) copy-start(bf16[2,48,2048]{2,1,0:T(8,128)(2,1)} %param.34) | copy-start | bytes 1179652
  36.5 14.4 %all-to-all-start.1 = ((bf16[32,56,128]{2,1,0:T(8,128)(2,1)}), bf16[32,56,128]{2,1,0:T(8,128)(2,1)S(1)}, u32[]{:S(2)}, u32[]{:S(2)}) async-start(bf16[32,56,128]{2,1,0:T(8,128)(2,1)} %attend.1), calls=%async_computation.1 | async-start | bytes 917504 | tf_op jit(solution)/shard_map/all_to_all | solution.py:267
  52.5 3.3 %collective-permute-start.10 = (bf16[16,56,128]{2,1,0:T(8,128)(2,1)}, bf16[16,56,128]{2,1,0:T(8,128)(2,1)S(1)}, u32[]{:S(2)}, u32[]{:S(2)}) collective-permute-start(bf16[16,56,128]{2,1,0:T(8,128)(2,1)} %get-tuple-element.138), channel_id=1, source_target_pairs={{0,256},{1,257},{2,258},{3,259},{4,260},{5,261},{6,262},{7,263},{8... | collective-permute-start | bytes 688136 | tf_op jit(solution)/shard_map/cond/branch_4_fun/ppermute | solution.py:242
  53.1 2.7 %collective-permute-start.11 = (bf16[16,56,128]{2,1,0:T(8,128)(2,1)}, bf16[16,56,128]{2,1,0:T(8,128)(2,1)S(1)}, u32[]{:S(2)}, u32[]{:S(2)}) collective-permute-start(bf16[16,56,128]{2,1,0:T(8,128)(2,1)} %get-tuple-element.139), channel_id=1, source_target_pairs={{0,128},{1,129},{2,130},{3,131},{4,132},{5,133},{6,134},{7,135},{8... | collective-permute-start | bytes 688136 | tf_op jit(solution)/shard_map/cond/branch_4_fun/ppermute | solution.py:242
  53.8 2.0 %collective-permute-start.12 = (bf16[16,56,128]{2,1,0:T(8,128)(2,1)}, bf16[16,56,128]{2,1,0:T(8,128)(2,1)S(1)}, u32[]{:S(2)}, u32[]{:S(2)}) collective-permute-start(bf16[16,56,128]{2,1,0:T(8,128)(2,1)} %get-tuple-element.140), channel_id=1, source_target_pairs={{0,128},{1,129},{2,130},{3,131},{4,132},{5,133},{6,134},{7,135},{8... | collective-permute-start | bytes 688136 | tf_op jit(solution)/shard_map/cond/branch_4_fun/ppermute | solution.py:242
  54.5 24.3 %collective-permute-start.9 = (bf16[16,56,128]{2,1,0:T(8,128)(2,1)}, bf16[16,56,128]{2,1,0:T(8,128)(2,1)S(1)}, u32[]{:S(2)}, u32[]{:S(2)}) collective-permute-start(bf16[16,56,128]{2,1,0:T(8,128)(2,1)} %get-tuple-element.137), channel_id=1, source_target_pairs={{0,384},{1,385},{2,386},{3,387},{4,388},{5,389},{6,390},{7,391},{8... | collective-permute-start | bytes 688136 | tf_op jit(solution)/shard_map/cond/branch_4_fun/ppermute | solution.py:242
  55.8 23.0 %copy-start.25 = (bf16[16,56,128]{2,1,0:T(8,128)(2,1)}, bf16[16,56,128]{2,1,0:T(8,128)(2,1)S(1)}, u32[]{:S(2)}) copy-start(bf16[16,56,128]{2,1,0:T(8,128)(2,1)S(1)} %collective-permute-done.10.refs_1_) | copy-start | bytes 688132 | tf_op jit(solution)/shard_map/cond
  55.8 23.0 %copy-start.28 = (bf16[16,56,128]{2,1,0:T(8,128)(2,1)}, bf16[16,56,128]{2,1,0:T(8,128)(2,1)S(1)}, u32[]{:S(2)}) copy-start(bf16[16,56,128]{2,1,0:T(8,128)(2,1)S(1)} %collective-permute-done.11.refs_2_) | copy-start | bytes 688132 | tf_op jit(solution)/shard_map/cond
  55.8 23.0 %copy-start.31 = (bf16[16,56,128]{2,1,0:T(8,128)(2,1)}, bf16[16,56,128]{2,1,0:T(8,128)(2,1)S(1)}, u32[]{:S(2)}) copy-start(bf16[16,56,128]{2,1,0:T(8,128)(2,1)S(1)} %collective-permute-done.12.refs_3_) | copy-start | bytes 688132 | tf_op jit(solution)/shard_map/cond
  78.8 0.7 copy-start.38

commit v3 on v2

--- a/solution.py
+++ b/solution.py
@@ -10,7 +10,8 @@
 
 HD = 128
 LOG2E = 1.4426950408889634
-VMEM_LIMIT = 48 * 2**20
+VMEM_LIMIT = 32 * 2**20
+SMALL = 16 * 2**20
 
 
 def lineages(slots):
@@ -117,41 +118,48 @@
     return packed.reshape(resident * heads, total, HD), facts
 
 
-def attend_kernel(x, out, q, k, v, *, rows, text, block):
+def attend_kernel(x, out, k, v, *, rows, text, peers):
     n = x.shape[0]
     video_rows, text_rows = n * rows, n * text
     total = video_rows + text_rows
     base = 3 * rows
-    for i, ref in enumerate((q, k, v)):
+    for i, ref in ((1, k), (2, v)):
         ref[0:video_rows, 0:HD] = x[:, i * rows : (i + 1) * rows, :].reshape(video_rows, HD)
         ref[video_rows:total, 0:HD] = x[:, base + i * text : base + (i + 1) * text, :].reshape(
             text_rows, HD
         )
     v[:, HD : 2 * HD] = jnp.ones((total, HD), v.dtype)
     scale = HD**-0.5 * LOG2E
-    for start in range(0, total, block):
-        piece = q[start : start + block, :]
-        scores = lax.dot_general(
+
+    blocks = [(i, i + peers, 0, 0, rows) for i in range(0, n, peers)] + [(0, n, base, rows, text)]
+
+    def scored(block):
+        first, last, source, _, count = block
+        piece = x[first:last, source : source + count, :].reshape((last - first) * count, HD)
+        return lax.dot_general(
             piece, k[...], (((1,), (1,)), ((), ())), preferred_element_type=jnp.float32
         )
+
+    scores = scored(blocks[0])
+    for i, (first, last, _, to, count) in enumerate(blocks):
+        ahead = scored(blocks[i + 1]) if i + 1 < len(blocks) else None
         row_max = jnp.max(scores, axis=1, keepdims=True)
         weights = jnp.exp2((scores - row_max) * scale).astype(v.dtype)
         summed = jnp.dot(weights, v[...], preferred_element_type=jnp.float32)
-        q[start : start + block, :] = (summed[:, :HD] / summed[:, HD:]).astype(q.dtype)
-    out[:, 0:rows, :] = q[0:video_rows, :].reshape(n, rows, HD)
-    out[:, rows : rows + text, :] = q[video_rows:total, :].reshape(n, text, HD)
-
-
-def attend(x, rows, text, block=256):
+        rounded = (summed[:, :HD] / summed[:, HD:]).astype(out.dtype)
+        out[first:last, to : to + count, :] = rounded.reshape(last - first, count, HD)
+        scores = ahead
+
+
+def attend(x, rows, text, peers=8):
     n = x.shape[0]
     total = n * (rows + text)
     return pl.pallas_call(
-        functools.partial(attend_kernel, rows=rows, text=text, block=block),
+        functools.partial(attend_kernel, rows=rows, text=text, peers=peers),
         in_specs=[pl.BlockSpec(memory_space=pltpu.VMEM)],
         out_specs=pl.BlockSpec(memory_space=pltpu.VMEM),
         out_shape=jax.ShapeDtypeStruct((n, rows + text, HD), x.dtype),
         scratch_shapes=[
-            pltpu.VMEM((total, HD), x.dtype),
             pltpu.VMEM((total, HD), x.dtype),
             pltpu.VMEM((total, 2 * HD), x.dtype),
         ],
@@ -182,6 +190,7 @@
         in_specs=[pl.BlockSpec(memory_space=pltpu.SMEM), vmem],
         out_specs=[vmem] * len(rounds),
         out_shape=[block] * len(rounds),
+        compiler_params=pltpu.CompilerParams(vmem_limit_bytes=SMALL),
         name="outgoing",
     )(facts, own)
 
@@ -232,6 +241,7 @@
             jax.ShapeDtypeStruct(noise.shape, noise.dtype),
             jax.ShapeDtypeStruct((slots, text, features), noise.dtype),
         ],
+        compiler_params=pltpu.CompilerParams(vmem_limit_bytes=SMALL),
         name="finish",
     )(facts, own, *received, noise)
 

time: 82.1 us -> 78.7 us (0.959)
  the two profiles are of different devices: /device:TPU:352 before, /device:TPU:65 now
where the time goes in v3:
time: 78.7 us; the launch traced here: 78.3 us
  waiting for transfers between devices  31.6 us (40%)
  blocking collectives  28.6 us (36%)
  Pallas kernels  9.29 us (12%)
  starting transfers between devices  6.93 us (9%)
  between operations  1.3 us (2%)
    all_to_all x1, blocking collectives, per_device(): lax.all_to_all(packed, 'seq', split_axis=0, concat_axis=0, tiled=True)  28.6 us
    ppermute x3, waiting for transfers between devices, resample(): lax.ppermute(send, 'dom', [m[:2] for m in members])  21.9 us
    all_to_all x1, waiting for transfers between devices, per_device(): lax.all_to_all(attended, 'seq', split_axis=0, concat_axis=0, tiled=True)  9.71 us
    pallas_call x1, Pallas kernels, attend(): pl.pallas_call(functools.partial(attend_kernel, rows=rows, text=text, pee...  4.72 us
    all_to_all x1, starting transfers between devices, per_device(): lax.all_to_all(attended, 'seq', split_axis=0, concat_axis=0, tiled=True)  3.67 us
    ppermute x3, starting transfers between devices, resample(): lax.ppermute(send, 'dom', [m[:2] for m in members])  3.26 us
    pallas_call x1, Pallas kernels, pack(): pl.pallas_call(functools.partial(pack_kernel, keys=keys), grid=(steps,),...  2.49 us
  transfers between devices with their start and end apart: 4, of which 3 were waited for; matrix products, arithmetic and copies ran while one was open for 1% of the time, Pallas kernels for 0%

profile of v3, /device:TPU:65, one launch (start us, length us, event | category | flops | bytes accessed | tf_op | source)
XLA Modules:
  0.0 78.3 jit_solution(323809351881112367)
XLA Ops:
  0.6 2.5 %pack.1 = (bf16[2,16,168,128]{3,2,1,0:T(8,128)(2,1)}, s32[10]{0:T(128)S(1)}) custom-call(s32[8]{0:T(128)} %counts.1, bf16[2,48,2048]{2,1,0:T(8,128)(2,1)} %vq.1, bf16[2,48,2048]{2,1,0:T(8,128)(2,1)} %vk.1, bf16[2,48,2048]{2,1,0:T(8,128)(2,1)} %vv.1, bf16[2,8,2048]{2,1,0:T(8,128)(2,1)} %tq.1, bf16[2,8,2048]{2,1,0:T(8,128)(2,1)} %tk.1, bf16[2,8,2048]{2,1,0:T(8,128)(2,1)} %tv.1), custom_call_target="tpu_custom_call" | custom-call | tf_op jit(solution)/shard_map/pack/pallas_call | solution.py:104
  3.1 28.6 %all_to_all.10.x = bf16[32,168,128]{2,1,0:T(8,128)(2,1)S(1)} all-to-all(bf16[32,168,128]{2,1,0:T(8,128)(2,1)} %bitcast.59), channel_id=1, replica_groups=mesh['dom'=4,'seq'=32,'rep'=4] {'seq'}, dimensions={0} | all-to-all | bytes 2752512 | tf_op jit(solution)/shard_map/all_to_all | solution.py:275
  31.8 0.0 copy-start
  31.8 4.7 %attend.1 = bf16[32,56,128]{2,1,0:T(8,128)(2,1)} custom-call(bf16[32,168,128]{2,1,0:T(8,128)(2,1)S(1)} %all_to_all.10.x), custom_call_target="tpu_custom_call" | custom-call | tf_op jit(solution)/shard_map/attend/pallas_call | solution.py:157
  36.5 3.7 %all-to-all-start.1 = ((bf16[32,56,128]{2,1,0:T(8,128)(2,1)}), bf16[32,56,128]{2,1,0:T(8,128)(2,1)S(1)}, u32[]{:S(2)}, u32[]{:S(2)}) async-start(bf16[32,56,128]{2,1,0:T(8,128)(2,1)} %attend.1), calls=%async_computation.1 | async-start | bytes 917504 | tf_op jit(solution)/shard_map/all_to_all | solution.py:277
  40.2 0.6 slice.3
  41.4 9.7 %all-to-all-done.1 = bf16[32,56,128]{2,1,0:T(8,128)(2,1)S(1)} async-done(((bf16[32,56,128]{2,1,0:T(8,128)(2,1)}), bf16[32,56,128]{2,1,0:T(8,128)(2,1)S(1)}, u32[]{:S(2)}, u32[]{:S(2)}) %all-to-all-start.1) | async-done | bytes 458784 | tf_op jit(solution)/shard_map/all_to_all | solution.py:277
  51.1 0.0 copy-done
  51.1 27.2 %conditional.1 = ((bf16[2,48,2048]{2,1,0:T(8,128)(2,1)}, bf16[2,8,2048]{2,1,0:T(8,128)(2,1)})) conditional(s32[]{:T(128)} %bitcast.19, (s32[10]{0:T(128)S(1)}, bf16[32,56,128]{2,1,0:T(8,128)(2,1)S(1)}, bf16[2,48,2048]{2,1,0:T(8,128)(2,1)S(1)}) %tuple.141, (s32[10]{0:T(128)S(1)}, bf16[32,56,128]{2,1,0:T(8,128)(2,1)S(1)}, ...), branch_computations={%region_0.0_spmd, %region_1.0_spmd, %region_2.0_spmd, %region_3.0_... | conditional | bytes 3670184 | solution.py:280
  51.1 0.6 outgoing.29
  51.7 1.3 %collective-permute-start.26 = (bf16[16,56,128]{2,1,0:T(8,128)(2,1)S(1)}, bf16[16,56,128]{2,1,0:T(8,128)(2,1)S(1)}, u32[]{:S(2)}, u32[]{:S(2)}) collective-permute-start(bf16[16,56,128]{2,1,0:T(8,128)(2,1)S(1)} %get-tuple-element.172), channel_id=1, source_target_pairs={{0,256},{128,384},{1,257},{129,385},{2,258},{130,386},{3,259},{131... | collective-permute-start | bytes 688136 | tf_op jit(solution)/shard_map/cond/branch_10_fun/ppermute | solution.py:252
  53.0 0.7 collective-permute-start.27
  53.7 1.3 %collective-permute-start.28 = (bf16[16,56,128]{2,1,0:T(8,128)(2,1)S(1)}, bf16[16,56,128]{2,1,0:T(8,128)(2,1)S(1)}, u32[]{:S(2)}, u32[]{:S(2)}) collective-permute-start(bf16[16,56,128]{2,1,0:T(8,128)(2,1)S(1)} %get-tuple-element.174), channel_id=1, source_target_pairs={{128,256},{129,257},{130,258},{131,259},{132,260},{133,261},{134,2... | collective-permute-start | bytes 688136 | tf_op jit(solution)/shard_map/cond/branch_10_fun/ppermute | solution.py:252
  55.0 6.9 %collective-permute-done.26.refs_0_ = bf16[16,56,128]{2,1,0:T(8,128)(2,1)S(1)} collective-permute-done((bf16[16,56,128]{2,1,0:T(8,128)(2,1)S(1)}, bf16[16,56,128]{2,1,0:T(8,128)(2,1)S(1)}, u32[]{:S(2)}, u32[]{:S(2)}) %collective-permute-start.26) | collective-permute-done | bytes 229408 | tf_op jit(solution)/shard_map/cond/branch_10_fun/ppermute | solution.py:252
  61.9 0.0 collective-permute-done.27.refs_1_
  61.9 15.0 %collective-permute-done.28.refs_2_ = bf16[16,56,128]{2,1,0:T(8,128)(2,1)S(1)} collective-permute-done((bf16[16,56,128]{2,1,0:T(8,128)(2,1)S(1)}, bf16[16,56,128]{2,1,0:T(8,128)(2,1)S(1)}, u32[]{:S(2)}, u32[]{:S(2)}) %collective-permute-start.28) | collective-permute-done | bytes 229408 | tf_op jit(solution)/shard_map/cond/branch_10_fun/ppermute | solution.py:252
  76.9 1.5 %finish.29 = (bf16[2,48,2048]{2,1,0:T(8,128)(2,1)}, bf16[2,8,2048]{2,1,0:T(8,128)(2,1)}) custom-call(s32[10]{0:T(128)S(1)} %get-tuple-element.170.facts, bf16[2,16,56,128]{3,2,1,0:T(8,128)(2,1)S(1)} %bitcast.42, bf16[16,56,128]{2,1,0:T(8,128)(2,1)S(1)} %collective-permute-done.26.refs_0_, bf16[16,56,128]{2,1,0:T(8,128)(2,1)S(1)} %collective-permute-done.27.refs_1_, ...), custom_call_target="tpu_custom_call" | custom-call | tf_op jit(solution)/shard_map/cond/branch_10_fun/finish/pallas_call | solution.py:236
Async XLA Ops:
  31.8 19.4 %copy-start = (bf16[2,48,2048]{2,1,0:T(8,128)(2,1)S(1)}, bf16[2,48,2048]{2,1,0:T(8,128)(2,1)}, u32[]{:S(2)}) copy-start(bf16[2,48,2048]{2,1,0:T(8,128)(2,1)} %param.34) | copy-start | bytes 1179652
  36.5 14.6 %all-to-all-start.1 = ((bf16[32,56,128]{2,1,0:T(8,128)(2,1)}), bf16[32,56,128]{2,1,0:T(8,128)(2,1)S(1)}, u32[]{:S(2)}, u32[]{:S(2)}) async-start(bf16[32,56,128]{2,1,0:T(8,128)(2,1)} %attend.1), calls=%async_computation.1 | async-start | bytes 917504 | tf_op jit(solution)/shard_map/all_to_all | solution.py:277
  51.7 10.2 %collective-permute-start.26 = (bf16[16,56,128]{2,1,0:T(8,128)(2,1)S(1)}, bf16[16,56,128]{2,1,0:T(8,128)(2,1)S(1)}, u32[]{:S(2)}, u32[]{:S(2)}) collective-permute-start(bf16[16,56,128]{2,1,0:T(8,128)(2,1)S(1)} %get-tuple-element.172), channel_id=1, source_target_pairs={{0,256},{128,384},{1,257},{129,385},{2,258},{130,386},{3,259},{131... | collective-permute-start | bytes 688136 | tf_op jit(solution)/shard_map/cond/branch_10_fun/ppermute | solution.py:252
  53.0 8.9 %collective-permute-start.27 = (bf16[16,56,128]{2,1,0:T(8,128)(2,1)S(1)}, bf16[16,56,128]{2,1,0:T(8,128)(2,1)S(1)}, u32[]{:S(2)}, u32[]{:S(2)}) collective-permute-start(bf16[16,56,128]{2,1,0:T(8,128)(2,1)S(1)} %get-tuple-element.173), channel_id=1, source_target_pairs={{128,384},{0,128},{129,385},{1,129},{130,386},{2,130},{131,387},{3... | collective-permute-start | bytes 688136 | tf_op jit(solution)/shard_map/cond/branch_10_fun/ppermute | solution.py:252
  53.7 23.2 %collective-permute-start.28 = (bf16[16,56,128]{2,1,0:T(8,128)(2,1)S(1)}, bf16[16,56,128]{2,1,0:T(8,128)(2,1)S(1)}, u32[]{:S(2)}, u32[]{:S(2)}) collective-permute-start(bf16[16,56,128]{2,1,0:T(8,128)(2,1)S(1)} %get-tuple-element.174), channel_id=1, source_target_pairs={{128,256},{129,257},{130,258},{131,259},{132,260},{133,261},{134,2... | collective-permute-start | bytes 688136 | tf_op jit(solution)/shard_map/cond/branch_10_fun/ppermute | solution.py:252

commit v4 on v3

--- a/solution.py
+++ b/solution.py
@@ -26,11 +26,19 @@
 
 
 def transfers(row):
-    pairs = []
-    for plane in range(1, len(row) // 2):
-        wanted = sorted(set(row[2 * plane : 2 * plane + 2]))
-        pairs += [(p // 2, plane) for p in wanted if p // 2 != plane]
-    return tuple(sorted(pairs))
+    moves, relays = [], []
+    planes = len(row) // 2
+    for plane in range(1, planes):
+        for slot in (2 * plane, 2 * plane + 1):
+            home = row[slot] // 2
+            if home == plane or (slot % 2 and row[slot] == row[slot - 1]):
+                continue
+            neighbours = [t for t in (slot // 2 * 2 - 2, slot // 2 * 2 - 1) if row[t] == row[slot]]
+            if plane == planes - 1 and home < plane - 1 and neighbours:
+                relays.append((slot, neighbours[0]))
+            else:
+                moves.append((home, plane, slot))
+    return tuple(moves), tuple(relays)
 
 
 def key_of(row):
@@ -43,79 +51,100 @@
         from_seven = as_int(row[7] // 2 == plane)
         same = as_int(row[6] == row[7])
         key = key + weight * (from_six + from_seven - from_six * same)
-    return key
+    return key + 144 * as_int(row[5] // 2 == 1) * as_int(row[5] == row[6])
+
+
+def links(move):
+    return set(range(min(move[:2]), max(move[:2])))
+
+
+def arrange(moves, relays):
+    fed = {t for _, t in relays}
+    order = sorted(moves, key=lambda m: (m[2] not in fed, -abs(m[1] - m[0])))
+    rounds = []
+    for move in order:
+        for i, members in enumerate(rounds):
+            apart = all(move[0] != m[0] and move[1] != m[1] for m in members)
+            clear = not any(m[2] in fed and links(m) & links(move) for m in members)
+            if apart and clear:
+                members.append(move)
+                break
+        else:
+            rounds.append([move])
+    return rounds
 
 
 def plans(slots):
     found = {}
     for row in lineages(slots):
         found[key_of(row)] = transfers(row)
-    out = []
-    for key in sorted(found):
-        rounds = []
-        seen = {}
-        for pair in sorted(found[key], key=lambda p: -abs(p[1] - p[0])):
-            which = seen.get(pair, 0)
-            seen[pair] = which + 1
-            for members in rounds:
-                if all(pair[0] != m[0] and pair[1] != m[1] for m in members):
-                    members.append(pair + (which,))
-                    break
-            else:
-                rounds.append([pair + (which,)])
-        out.append((key, rounds))
-    return out
-
-
-def pack_kernel(counts, vq, vk, vv, tq, tk, tv, out, facts, *, keys):
-    @pl.when(pl.program_id(0) == 0)
-    def _():
-        slots = counts.shape[0]
-        running = [counts[0]]
-        for i in range(1, slots):
-            running.append(running[-1] + counts[i])
-        row = [sum(jnp.where(r <= j, 1, 0) for r in running) for j in range(slots)]
-        facts[0] = lax.axis_index("dom")
-        for j in range(slots):
-            facts[1 + j] = row[j]
-        key = key_of(row)
-        facts[1 + slots] = sum(jnp.where(key == k, i, 0) for i, k in enumerate(keys))
-
-    rows, text = vq.shape[1], tq.shape[1]
-    base = 3 * rows
-    for p in range(vq.shape[0]):
-        for h in range(vq.shape[2] // HD):
-            columns = slice(h * HD, (h + 1) * HD)
-            for i, ref in enumerate((vq, vk, vv)):
-                out[p, h, i * rows : (i + 1) * rows, :] = ref[p, :, columns]
-            for i, ref in enumerate((tq, tk, tv)):
-                out[p, h, base + i * text : base + (i + 1) * text, :] = ref[p, :, columns]
-
-
-def pack(counts, vq, vk, vv, tq, tk, tv, keys, steps=2):
-    resident, rows, features = vq.shape
-    text = tq.shape[1]
-    heads = features // HD
-    width = features // steps
-    total = 3 * (rows + text)
-    video = pl.BlockSpec((resident, rows, width), lambda i: (0, 0, i))
-    words = pl.BlockSpec((resident, text, width), lambda i: (0, 0, i))
+    return [(key, arrange(*found[key]), found[key][1]) for key in sorted(found)]
+
+
+def pack_kernel(*refs, pieces):
+    arrays, out, held, sems = refs[:6], refs[6], refs[7:13], refs[13]
+    width = arrays[0].shape[2] // pieces
+
+    def copies(piece):
+        columns = pl.ds(piece * width, width)
+        return [
+            pltpu.make_async_copy(ref.at[:, :, columns], to.at[:, :, columns], sems.at[piece, i])
+            for i, (ref, to) in enumerate(zip(arrays, held))
+        ]
+
+    for piece in range(pieces):
+        for copy in copies(piece):
+            copy.start()
+    for piece in range(pieces):
+        for copy in copies(piece):
+            copy.wait()
+        for p in range(out.shape[0]):
+            for h in range(piece * width // HD, (piece + 1) * width // HD):
+                at = 0
+                for ref in held:
+                    out[p, h, at : at + ref.shape[1], :] = ref[p, :, h * HD : (h + 1) * HD]
+                    at += ref.shape[1]
+
+
+def pack(arrays, pieces=4):
+    resident, rows, features = arrays[0].shape
+    text = arrays[3].shape[1]
+    shape = (resident, features // HD, 3 * (rows + text), HD)
+    packed = pl.pallas_call(
+        functools.partial(pack_kernel, pieces=pieces),
+        in_specs=[pl.BlockSpec(memory_space=pl.ANY)] * 6,
+        out_specs=pl.BlockSpec(memory_space=pltpu.VMEM),
+        out_shape=jax.ShapeDtypeStruct(shape, arrays[0].dtype),
+        scratch_shapes=[pltpu.VMEM(a.shape, a.dtype) for a in arrays]
+        + [pltpu.SemaphoreType.DMA((pieces, 6))],
+        compiler_params=pltpu.CompilerParams(vmem_limit_bytes=SMALL),
+        name="pack",
+    )(*[pltpu.with_memory_space_constraint(a, pltpu.HBM) for a in arrays])
+    return packed.reshape((-1,) + shape[2:])
+
+
+def facts_kernel(counts, _, facts, *, keys):
+    slots = counts.shape[0]
+    running = [counts[0]]
+    for i in range(1, slots):
+        running.append(running[-1] + counts[i])
+    row = [sum(jnp.where(r <= j, 1, 0) for r in running) for j in range(slots)]
+    facts[0] = lax.axis_index("dom")
+    for j in range(slots):
+        facts[1 + j] = row[j]
+    key = key_of(row)
+    facts[1 + slots] = sum(jnp.where(key == k, i, 0) for i, k in enumerate(keys))
+
+
+def find_facts(counts, after, keys):
     scalars = pl.BlockSpec(memory_space=pltpu.SMEM)
-    packed, facts = pl.pallas_call(
-        functools.partial(pack_kernel, keys=keys),
-        grid=(steps,),
-        in_specs=[scalars] + [video] * 3 + [words] * 3,
-        out_specs=[
-            pl.BlockSpec((resident, heads // steps, total, HD), lambda i: (0, i, 0, 0)),
-            scalars,
-        ],
-        out_shape=[
-            jax.ShapeDtypeStruct((resident, heads, total, HD), vq.dtype),
-            jax.ShapeDtypeStruct((counts.shape[0] + 2,), jnp.int32),
-        ],
-        name="pack",
-    )(counts, vq, vk, vv, tq, tk, tv)
-    return packed.reshape(resident * heads, total, HD), facts
+    return pl.pallas_call(
+        functools.partial(facts_kernel, keys=keys),
+        in_specs=[scalars, pl.BlockSpec(memory_space=pl.ANY)],
+        out_specs=scalars,
+        out_shape=jax.ShapeDtypeStruct((counts.shape[0] + 2,), jnp.int32),
+        name="facts",
+    )(counts, after)
 
 
 def attend_kernel(x, out, k, v, *, rows, text, peers):
@@ -172,13 +201,8 @@
     dom = facts[0]
     for members, send in zip(rounds, sends):
         index = 0
-        for source, target, which in members:
-            slot = 1 + 2 * target
-            if which == 0:
-                wanted = jnp.where(facts[slot] // 2 == source, facts[slot], facts[slot + 1])
-            else:
-                wanted = facts[slot + 1]
-            index = jnp.where(dom == source, lax.rem(wanted, 2), index)
+        for source, _, slot in members:
+            index = jnp.where(dom == source, lax.rem(facts[1 + slot], 2), index)
         send[...] = own[index]
 
 
@@ -195,21 +219,22 @@
     )(facts, own)
 
 
-def finish_kernel(facts, own, *refs, rounds):
+def finish_kernel(facts, own, *refs, places):
     received, (noise, video, words) = refs[:-3], refs[-3:]
     slots, rows = noise.shape[0], noise.shape[1]
     text = words.shape[1]
     dom = facts[0]
+    chosen = 0
     for s in range(slots):
-        ancestor = facts[1 + 2 * dom + s]
-        origin = ancestor // 2
+        ancestor = facts[1 + slots * dom + s]
+        before = chosen
         chosen = 0
-        for r, members in enumerate(rounds):
-            for source, target, which in members:
-                twice = sum(m[:2] == (source, target) for ms in rounds for m in ms) == 2
-                if not twice or which == s:
-                    hit = jnp.logical_and(dom == target, origin == source)
-                    chosen = jnp.where(hit, 1 + r, chosen)
+        for slot, r in places:
+            if slot % slots == s:
+                chosen = jnp.where(dom == slot // slots, 1 + r, chosen)
+        if s:
+            chosen = jnp.where(ancestor == facts[slots * dom + s], before, chosen)
+        chosen = jnp.where(ancestor // slots == dom, 0, chosen)
 
         def write(block, s=s):
             for h in range(own.shape[1]):
@@ -221,7 +246,7 @@
 
         @pl.when(chosen == 0)
         def _(write=write, ancestor=ancestor):
-            write(own.at[lax.rem(ancestor, 2)])
+            write(own.at[lax.rem(ancestor, slots)])
 
         for r, block in enumerate(received):
 
@@ -230,11 +255,11 @@
                 write(block)
 
 
-def finish(facts, own, received, noise, text, rounds):
+def finish(facts, own, received, noise, text, places):
     slots, _, features = noise.shape
     vmem = pl.BlockSpec(memory_space=pltpu.VMEM)
     return pl.pallas_call(
-        functools.partial(finish_kernel, rounds=rounds),
+        functools.partial(finish_kernel, places=places),
         in_specs=[pl.BlockSpec(memory_space=pltpu.SMEM)] + [vmem] * (2 + len(received)),
         out_specs=[vmem, vmem],
         out_shape=[
@@ -246,12 +271,18 @@
     )(facts, own, *received, noise)
 
 
-def resample(rounds, text, facts, own, noise):
+def resample(rounds, relays, text, facts, own, noise):
     sends = outgoing(facts, own, rounds)
     received = [
         lax.ppermute(send, "dom", [m[:2] for m in members]) for send, members in zip(sends, rounds)
     ]
-    return tuple(finish(facts, own, received, noise, text, rounds))
+    places = [(m[2], r) for r, members in enumerate(rounds) for m in members]
+    held = dict(places)
+    for slot, neighbour in relays:
+        places.append((slot, len(received)))
+        hop = (neighbour // 2, slot // 2)
+        received.append(lax.ppermute(received[held[neighbour]], "dom", [hop]))
+    return tuple(finish(facts, own, received, noise, text, places))
 
 
 def per_device(
@@ -262,21 +293,15 @@
     heads = features // HD
     known = plans(counts.shape[0])
 
-    packed, facts = pack(
-        counts,
-        video_query,
-        video_key,
-        video_value,
-        text_query,
-        text_key,
-        text_value,
-        [key for key, _ in known],
+    packed = pack(
+        (video_query, video_key, video_value, text_query, text_key, text_value)
     )
     gathered = lax.all_to_all(packed, "seq", split_axis=0, concat_axis=0, tiled=True)
     attended = attend(gathered, rows, text)
+    facts = find_facts(counts, attended, [plan[0] for plan in known])
     returned = lax.all_to_all(attended, "seq", split_axis=0, concat_axis=0, tiled=True)
     own = returned.reshape(resident, heads, rows + text, HD)
-    branches = [functools.partial(resample, rounds, text) for _, rounds in known]
+    branches = [functools.partial(resample, *plan[1:], text) for plan in known]
     return lax.switch(facts[counts.shape[0] + 1], branches, facts, own, fresh_noise)
 
 

time: 78.7 us -> 72.8 us (0.925)
  waiting for transfers between devices: 31.6 us -> 23.7 us
  starting transfers between devices: 6.93 us -> 8.51 us
    ppermute x3 -> x2, waiting for transfers between devices: 21.9 us -> 15.4 us  [resample(): lax.ppermute(send, 'dom', [m[:2] for m in members])]
    ppermute x3 -> x2, starting transfers between devices: 3.26 us -> 4.83 us  [resample(): lax.ppermute(send, 'dom', [m[:2] for m in members])]
    all_to_all x1, waiting for transfers between devices: 9.71 us -> 8.33 us  [per_device(): lax.all_to_all(attended, 'seq', split_axis=0, concat_axis=0, tiled=True)]
    pallas_call x2 -> x3, Pallas kernels: 3.96 us -> 4.52 us  [the longest x1 1.69 us: pack(): pl.pallas_call(functools.partial(pack_kernel, pieces=pieces), in_specs=[p...]
  transfers between devices with their start and end apart: 4 -> 3, of which waited for: 3 -> 3; matrix products, arithmetic and copies ran while one was open for 1% -> 1% of each run, Pallas kernels for 0% -> 2%
where the time goes in v4:
time: 72.8 us; the launch traced here: 72.5 us
  blocking collectives  28.4 us (39%)
  waiting for transfers between devices  23.7 us (33%)
  Pallas kernels  9.85 us (14%)
  starting transfers between devices  8.51 us (12%)
  between operations  1.31 us (2%)
    all_to_all x1, blocking collectives, per_device(): lax.all_to_all(packed, 'seq', split_axis=0, concat_axis=0, tiled=True)  28.4 us
    ppermute x2, waiting for transfers between devices, resample(): lax.ppermute(send, 'dom', [m[:2] for m in members])  15.4 us
    all_to_all x1, waiting for transfers between devices, per_device(): lax.all_to_all(attended, 'seq', split_axis=0, concat_axis=0, tiled=True)  8.33 us
    ppermute x2, starting transfers between devices, resample(): lax.ppermute(send, 'dom', [m[:2] for m in members])  4.83 us
    pallas_call x1, Pallas kernels, attend(): pl.pallas_call(functools.partial(attend_kernel, rows=rows, text=text, pee...  4.75 us
    all_to_all x1, starting transfers between devices, per_device(): lax.all_to_all(attended, 'seq', split_axis=0, concat_axis=0, tiled=True)  3.67 us
    pallas_call x1, Pallas kernels, pack(): pl.pallas_call(functools.partial(pack_kernel, pieces=pieces), in_specs=[p...  1.69 us
  transfers between devices with their start and end apart: 3, of which 3 were waited for; matrix products, arithmetic and copies ran while one was open for 1% of the time, Pallas kernels for 2%

profile of v4, /device:TPU:65, one launch (start us, length us, event | category | flops | bytes accessed | tf_op | source)
XLA Modules:
  0.0 72.5 jit_solution(12885978616113241832)
XLA Ops:
  0.6 1.7 %pack.1 = bf16[2,16,168,128]{3,2,1,0:T(8,128)(2,1)S(1)} custom-call(bf16[2,48,2048]{2,1,0:T(8,128)(2,1)} %refs_0_.1, bf16[2,48,2048]{2,1,0:T(8,128)(2,1)} %refs_1_.1, bf16[2,48,2048]{2,1,0:T(8,128)(2,1)} %refs_2_.1, bf16[2,8,2048]{2,1,0:T(8,128)(2,1)} %refs_3_.1, bf16[2,8,2048]{2,1,0:T(8,128)(2,1)} %refs_4_.1, bf16[2,8,2048]{2,1,0:T(8,128)(2,1)} %refs_5_.1), custom_call_target="tpu_custom_call" | custom-call | tf_op jit(solution)/shard_map/pack/pallas_call | solution.py:113
  2.3 28.4 %all_to_all.10.x = bf16[32,168,128]{2,1,0:T(8,128)(2,1)S(1)} all-to-all(bf16[32,168,128]{2,1,0:T(8,128)(2,1)S(1)} %bitcast.23), channel_id=1, replica_groups=mesh['dom'=4,'seq'=32,'rep'=4] {'seq'}, dimensions={0} | all-to-all | bytes 2752512 | tf_op jit(solution)/shard_map/all_to_all | solution.py:299
  30.8 0.0 copy-start
  30.8 4.7 %attend.1._ = bf16[32,56,128]{2,1,0:T(8,128)(2,1)} custom-call(bf16[32,168,128]{2,1,0:T(8,128)(2,1)S(1)} %all_to_all.10.x), custom_call_target="tpu_custom_call" | custom-call | tf_op jit(solution)/shard_map/attend/pallas_call | solution.py:186
  35.5 3.7 %all-to-all-start.1 = ((bf16[32,56,128]{2,1,0:T(8,128)(2,1)}), bf16[32,56,128]{2,1,0:T(8,128)(2,1)S(1)}, u32[]{:S(2)}, u32[]{:S(2)}) async-start(bf16[32,56,128]{2,1,0:T(8,128)(2,1)} %attend.1._), calls=%async_computation.1 | async-start | bytes 917504 | tf_op jit(solution)/shard_map/all_to_all | solution.py:302
  39.2 1.4 %facts.1 = s32[10]{0:T(128)S(1)} custom-call(s32[8]{0:T(128)} %counts.1, bf16[32,56,128]{2,1,0:T(8,128)(2,1)} %attend.1._), custom_call_target="tpu_custom_call" | custom-call | tf_op jit(solution)/shard_map/facts/pallas_call | solution.py:141
  40.6 0.6 slice.3
  41.8 8.3 %all-to-all-done.1 = bf16[32,56,128]{2,1,0:T(8,128)(2,1)S(1)} async-done(((bf16[32,56,128]{2,1,0:T(8,128)(2,1)}), bf16[32,56,128]{2,1,0:T(8,128)(2,1)S(1)}, u32[]{:S(2)}, u32[]{:S(2)}) %all-to-all-start.1) | async-done | bytes 458784 | tf_op jit(solution)/shard_map/all_to_all | solution.py:302
  50.1 0.0 copy-done
  50.1 22.3 %conditional.1 = ((bf16[2,48,2048]{2,1,0:T(8,128)(2,1)}, bf16[2,8,2048]{2,1,0:T(8,128)(2,1)})) conditional(s32[]{:T(128)} %bitcast.22, (s32[10]{0:T(128)S(1)}, bf16[32,56,128]{2,1,0:T(8,128)(2,1)S(1)}, bf16[2,48,2048]{2,1,0:T(8,128)(2,1)S(1)}) %tuple.155, (s32[10]{0:T(128)S(1)}, bf16[32,56,128]{2,1,0:T(8,128)(2,1)S(1)}, ...), branch_computations={%region_0.0_spmd, %region_1.0_spmd, %region_2.0_spmd, %region_3.0_... | conditional | bytes 3670184 | solution.py:305
  50.1 0.6 outgoing.36
  50.7 1.3 %collective-permute-start.39 = (bf16[16,56,128]{2,1,0:T(8,128)(2,1)S(1)}, bf16[16,56,128]{2,1,0:T(8,128)(2,1)S(1)}, u32[]{:S(2)}, u32[]{:S(2)}) collective-permute-start(bf16[16,56,128]{2,1,0:T(8,128)(2,1)S(1)} %get-tuple-element.206), channel_id=1, source_target_pairs={{0,256},{128,384},{1,257},{129,385},{2,258},{130,386},{3,259},{131... | collective-permute-start | bytes 688136 | tf_op jit(solution)/shard_map/cond/branch_15_fun/ppermute | solution.py:277
  52.0 3.5 %collective-permute-start.40 = (bf16[16,56,128]{2,1,0:T(8,128)(2,1)S(1)}, bf16[16,56,128]{2,1,0:T(8,128)(2,1)S(1)}, u32[]{:S(2)}, u32[]{:S(2)}) collective-permute-start(bf16[16,56,128]{2,1,0:T(8,128)(2,1)S(1)} %get-tuple-element.207), channel_id=1, source_target_pairs={{0,128},{128,256},{256,384},{1,129},{129,257},{257,385},{2,130},{1... | collective-permute-start | bytes 688136 | tf_op jit(solution)/shard_map/cond/branch_15_fun/ppermute | solution.py:277
  55.6 5.3 %collective-permute-done.39.refs_0_ = bf16[16,56,128]{2,1,0:T(8,128)(2,1)S(1)} collective-permute-done((bf16[16,56,128]{2,1,0:T(8,128)(2,1)S(1)}, bf16[16,56,128]{2,1,0:T(8,128)(2,1)S(1)}, u32[]{:S(2)}, u32[]{:S(2)}) %collective-permute-start.39) | collective-permute-done | bytes 229408 | tf_op jit(solution)/shard_map/cond/branch_15_fun/ppermute | solution.py:277
  60.9 10.1 %collective-permute-done.40.refs_1_ = bf16[16,56,128]{2,1,0:T(8,128)(2,1)S(1)} collective-permute-done((bf16[16,56,128]{2,1,0:T(8,128)(2,1)S(1)}, bf16[16,56,128]{2,1,0:T(8,128)(2,1)S(1)}, u32[]{:S(2)}, u32[]{:S(2)}) %collective-permute-start.40) | collective-permute-done | bytes 229408 | tf_op jit(solution)/shard_map/cond/branch_15_fun/ppermute | solution.py:277
  71.0 1.5 %finish.36 = (bf16[2,48,2048]{2,1,0:T(8,128)(2,1)}, bf16[2,8,2048]{2,1,0:T(8,128)(2,1)}) custom-call(s32[10]{0:T(128)S(1)} %get-tuple-element.204.facts, bf16[2,16,56,128]{3,2,1,0:T(8,128)(2,1)S(1)} %bitcast.55, bf16[16,56,128]{2,1,0:T(8,128)(2,1)S(1)} %collective-permute-done.39.refs_0_, bf16[16,56,128]{2,1,0:T(8,128)(2,1)S(1)} %collective-permute-done.40.refs_1_, ...), custom_call_target="tpu_custom_call" | custom-call | tf_op jit(solution)/shard_map/cond/branch_15_fun/finish/pallas_call | solution.py:261
Async XLA Ops:
  30.8 19.4 %copy-start = (bf16[2,48,2048]{2,1,0:T(8,128)(2,1)S(1)}, bf16[2,48,2048]{2,1,0:T(8,128)(2,1)}, u32[]{:S(2)}) copy-start(bf16[2,48,2048]{2,1,0:T(8,128)(2,1)} %param.36) | copy-start | bytes 1179652
  35.5 14.6 %all-to-all-start.1 = ((bf16[32,56,128]{2,1,0:T(8,128)(2,1)}), bf16[32,56,128]{2,1,0:T(8,128)(2,1)S(1)}, u32[]{:S(2)}, u32[]{:S(2)}) async-start(bf16[32,56,128]{2,1,0:T(8,128)(2,1)} %attend.1._), calls=%async_computation.1 | async-start | bytes 917504 | tf_op jit(solution)/shard_map/all_to_all | solution.py:302
  50.7 10.2 %collective-permute-start.39 = (bf16[16,56,128]{2,1,0:T(8,128)(2,1)S(1)}, bf16[16,56,128]{2,1,0:T(8,128)(2,1)S(1)}, u32[]{:S(2)}, u32[]{:S(2)}) collective-permute-start(bf16[16,56,128]{2,1,0:T(8,128)(2,1)S(1)} %get-tuple-element.206), channel_id=1, source_target_pairs={{0,256},{128,384},{1,257},{129,385},{2,258},{130,386},{3,259},{131... | collective-permute-start | bytes 688136 | tf_op jit(solution)/shard_map/cond/branch_15_fun/ppermute | solution.py:277
  52.0 19.0 %collective-permute-start.40 = (bf16[16,56,128]{2,1,0:T(8,128)(2,1)S(1)}, bf16[16,56,128]{2,1,0:T(8,128)(2,1)S(1)}, u32[]{:S(2)}, u32[]{:S(2)}) collective-permute-start(bf16[16,56,128]{2,1,0:T(8,128)(2,1)S(1)} %get-tuple-element.207), channel_id=1, source_target_pairs={{0,128},{128,256},{256,384},{1,129},{129,257},{257,385},{2,130},{1... | collective-permute-start | bytes 688136 | tf_op jit(solution)/shard_map/cond/branch_15_fun/ppermute | solution.py:277

commit v5 on v4

--- a/solution.py
+++ b/solution.py
@@ -28,13 +28,15 @@
 def transfers(row):
     moves, relays = [], []
     planes = len(row) // 2
+    last = planes - 1
+    both = row[-2] // 2 == row[-1] // 2 and row[-2] != row[-1]
     for plane in range(1, planes):
         for slot in (2 * plane, 2 * plane + 1):
             home = row[slot] // 2
             if home == plane or (slot % 2 and row[slot] == row[slot - 1]):
                 continue
-            neighbours = [t for t in (slot // 2 * 2 - 2, slot // 2 * 2 - 1) if row[t] == row[slot]]
-            if plane == planes - 1 and home < plane - 1 and neighbours:
+            neighbours = [t for t in (2 * last - 2, 2 * last - 1) if row[t] == row[slot]]
+            if plane == last and neighbours and (home == 0 or (home == 1 and both)):
                 relays.append((slot, neighbours[0]))
             else:
                 moves.append((home, plane, slot))
@@ -51,7 +53,8 @@
         from_seven = as_int(row[7] // 2 == plane)
         same = as_int(row[6] == row[7])
         key = key + weight * (from_six + from_seven - from_six * same)
-    return key + 144 * as_int(row[5] // 2 == 1) * as_int(row[5] == row[6])
+    shared = as_int(row[5] // 2 == 1) * as_int(row[5] == row[6])
+    return key + 144 * shared * as_int(row[6] != row[7]) * as_int(row[7] // 2 == 1)
 
 
 def links(move):
@@ -60,18 +63,24 @@
 
 def arrange(moves, relays):
     fed = {t for _, t in relays}
-    order = sorted(moves, key=lambda m: (m[2] not in fed, -abs(m[1] - m[0])))
-    rounds = []
-    for move in order:
-        for i, members in enumerate(rounds):
-            apart = all(move[0] != m[0] and move[1] != m[1] for m in members)
-            clear = not any(m[2] in fed and links(m) & links(move) for m in members)
-            if apart and clear:
-                members.append(move)
-                break
-        else:
-            rounds.append([move])
-    return rounds
+    for count in range(1, len(moves) + 1):
+        best = None
+        for numbers in itertools.product(range(count), repeat=len(moves)):
+            rounds = [[m for m, i in zip(moves, numbers) if i == r] for r in range(count)]
+            if any(len({m[end] for m in ms}) < len(ms) for ms in rounds for end in (0, 1)):
+                continue
+            if not fed <= {m[2] for m in rounds[0]}:
+                continue
+            loads = [[sum(k in links(m) for m in ms) for k in range(8)] for ms in rounds]
+            if any(loads[0][k] > 1 for m in rounds[0] if m[2] in fed for k in links(m)):
+                continue
+            early = sum(i * (4 - len(links(m))) for m, i in zip(moves, numbers))
+            rank = (sum(max(load) for load in loads), early, numbers)
+            if best is None or rank < best[0]:
+                best = (rank, rounds)
+        if best is not None:
+            return best[1]
+    return []
 
 
 def plans(slots):
@@ -106,7 +115,7 @@
                     at += ref.shape[1]
 
 
-def pack(arrays, pieces=4):
+def pack(arrays, pieces=1):
     resident, rows, features = arrays[0].shape
     text = arrays[3].shape[1]
     shape = (resident, features // HD, 3 * (rows + text), HD)

time: 72.8 us -> 72.8 us (level)
  the two profiles are of different devices: /device:TPU:65 before, /device:TPU:160 now
where the time goes in v5:
time: 72.8 us; the launch traced here: 72.5 us
  blocking collectives  27.8 us (38%)
  waiting for transfers between devices  21.4 us (29%)
  starting transfers between devices  11.7 us (16%)
  Pallas kernels  9.7 us (13%)
  between operations  1.31 us (2%)
    all_to_all x1, blocking collectives, per_device(): lax.all_to_all(packed, 'seq', split_axis=0, concat_axis=0, tiled=True)  27.8 us
    ppermute x3, waiting for transfers between devices, resample(): lax.ppermute(send, 'dom', [m[:2] for m in members])  13.5 us
    all_to_all x1, waiting for transfers between devices, per_device(): lax.all_to_all(attended, 'seq', split_axis=0, concat_axis=0, tiled=True)  7.93 us
    ppermute x3, starting transfers between devices, resample(): lax.ppermute(send, 'dom', [m[:2] for m in members])  7.14 us
    pallas_call x1, Pallas kernels, attend(): pl.pallas_call(functools.partial(attend_kernel, rows=rows, text=text, pee...  4.73 us
    all_to_all x1, starting transfers between devices, per_device(): lax.all_to_all(attended, 'seq', split_axis=0, concat_axis=0, tiled=True)  3.88 us
    pallas_call x1, Pallas kernels, pack(): pl.pallas_call(functools.partial(pack_kernel, pieces=pieces), in_specs=[p...  1.53 us
    pallas_call x1, Pallas kernels, finish(): pl.pallas_call(functools.partial(finish_kernel, places=places), in_specs=...  1.47 us
  transfers between devices with their start and end apart: 5, of which 3 were waited for; matrix products, arithmetic and copies ran while one was open for 1% of the time, Pallas kernels for 2%

profile of v5, /device:TPU:160, one launch (start us, length us, event | category | flops | bytes accessed | tf_op | source)
XLA Modules:
  0.0 72.5 jit_solution(7162773561499638275)
XLA Ops:
  0.6 1.5 %pack.1 = bf16[2,16,168,128]{3,2,1,0:T(8,128)(2,1)S(1)} custom-call(bf16[2,48,2048]{2,1,0:T(8,128)(2,1)} %refs_0_.1, bf16[2,48,2048]{2,1,0:T(8,128)(2,1)} %refs_1_.1, bf16[2,48,2048]{2,1,0:T(8,128)(2,1)} %refs_2_.1, bf16[2,8,2048]{2,1,0:T(8,128)(2,1)} %refs_3_.1, bf16[2,8,2048]{2,1,0:T(8,128)(2,1)} %refs_4_.1, bf16[2,8,2048]{2,1,0:T(8,128)(2,1)} %refs_5_.1), custom_call_target="tpu_custom_call" | custom-call | tf_op jit(solution)/shard_map/pack/pallas_call | solution.py:122
  2.2 27.8 %all_to_all.10.x = bf16[32,168,128]{2,1,0:T(8,128)(2,1)S(1)} all-to-all(bf16[32,168,128]{2,1,0:T(8,128)(2,1)S(1)} %bitcast.21), channel_id=1, replica_groups=mesh['dom'=4,'seq'=32,'rep'=4] {'seq'}, dimensions={0} | all-to-all | bytes 2752512 | tf_op jit(solution)/shard_map/all_to_all | solution.py:308
  29.9 0.0 copy-start
  29.9 4.7 %attend.1._ = bf16[32,56,128]{2,1,0:T(8,128)(2,1)} custom-call(bf16[32,168,128]{2,1,0:T(8,128)(2,1)S(1)} %all_to_all.10.x), custom_call_target="tpu_custom_call" | custom-call | tf_op jit(solution)/shard_map/attend/pallas_call | solution.py:195
  34.7 3.9 %all-to-all-start.1 = ((bf16[32,56,128]{2,1,0:T(8,128)(2,1)}), bf16[32,56,128]{2,1,0:T(8,128)(2,1)S(1)}, u32[]{:S(2)}, u32[]{:S(2)}) async-start(bf16[32,56,128]{2,1,0:T(8,128)(2,1)} %attend.1._), calls=%async_computation.1 | async-start | bytes 917504 | tf_op jit(solution)/shard_map/all_to_all | solution.py:311
  38.6 1.4 %facts.1 = s32[10]{0:T(128)S(1)} custom-call(s32[8]{0:T(128)} %counts.1, bf16[32,56,128]{2,1,0:T(8,128)(2,1)} %attend.1._), custom_call_target="tpu_custom_call" | custom-call | tf_op jit(solution)/shard_map/facts/pallas_call | solution.py:150
  40.0 0.6 slice.3
  41.2 7.9 %all-to-all-done.1 = bf16[32,56,128]{2,1,0:T(8,128)(2,1)S(1)} async-done(((bf16[32,56,128]{2,1,0:T(8,128)(2,1)}), bf16[32,56,128]{2,1,0:T(8,128)(2,1)S(1)}, u32[]{:S(2)}, u32[]{:S(2)}) %all-to-all-start.1) | async-done | bytes 458784 | tf_op jit(solution)/shard_map/all_to_all | solution.py:311
  49.1 0.0 copy-done
  49.1 23.4 %conditional.1 = ((bf16[2,48,2048]{2,1,0:T(8,128)(2,1)}, bf16[2,8,2048]{2,1,0:T(8,128)(2,1)})) conditional(s32[]{:T(128)} %bitcast.20, (s32[10]{0:T(128)S(1)}, bf16[32,56,128]{2,1,0:T(8,128)(2,1)S(1)}, bf16[2,48,2048]{2,1,0:T(8,128)(2,1)S(1)}) %tuple.141, (s32[10]{0:T(128)S(1)}, bf16[32,56,128]{2,1,0:T(8,128)(2,1)S(1)}, ...), branch_computations={%region_0.0_spmd, %region_1.0_spmd, %region_2.0_spmd, %region_3.0_... | conditional | bytes 3670184 | solution.py:314
  49.1 0.6 outgoing.27
  49.7 0.7 collective-permute-start.20
  50.4 5.2 %collective-permute-start.21 = (bf16[16,56,128]{2,1,0:T(8,128)(2,1)S(1)}, bf16[16,56,128]{2,1,0:T(8,128)(2,1)S(1)}, u32[]{:S(2)}, u32[]{:S(2)}) collective-permute-start(bf16[16,56,128]{2,1,0:T(8,128)(2,1)S(1)} %get-tuple-element.158), channel_id=1, source_target_pairs={{0,128},{128,384},{1,129},{129,385},{2,130},{130,386},{3,131},{131... | collective-permute-start | bytes 688136 | tf_op jit(solution)/shard_map/cond/branch_8_fun/ppermute | solution.py:286
  55.6 1.3 %collective-permute-start.22 = (bf16[16,56,128]{2,1,0:T(8,128)(2,1)S(1)}, bf16[16,56,128]{2,1,0:T(8,128)(2,1)S(1)}, u32[]{:S(2)}, u32[]{:S(2)}) collective-permute-start(bf16[16,56,128]{2,1,0:T(8,128)(2,1)S(1)} %get-tuple-element.159), channel_id=1, source_target_pairs={{0,128},{1,129},{2,130},{3,131},{4,132},{5,133},{6,134},{7,135},{8... | collective-permute-start | bytes 688136 | tf_op jit(solution)/shard_map/cond/branch_8_fun/ppermute | solution.py:286
  56.9 0.0 collective-permute-done.20.refs_0_
  56.9 0.7 collective-permute-start.23
  57.6 8.8 %collective-permute-done.21.refs_1_ = bf16[16,56,128]{2,1,0:T(8,128)(2,1)S(1)} collective-permute-done((bf16[16,56,128]{2,1,0:T(8,128)(2,1)S(1)}, bf16[16,56,128]{2,1,0:T(8,128)(2,1)S(1)}, u32[]{:S(2)}, u32[]{:S(2)}) %collective-permute-start.21) | collective-permute-done | bytes 229408 | tf_op jit(solution)/shard_map/cond/branch_8_fun/ppermute | solution.py:286
  66.4 4.6 %collective-permute-done.22.refs_2_ = bf16[16,56,128]{2,1,0:T(8,128)(2,1)S(1)} collective-permute-done((bf16[16,56,128]{2,1,0:T(8,128)(2,1)S(1)}, bf16[16,56,128]{2,1,0:T(8,128)(2,1)S(1)}, u32[]{:S(2)}, u32[]{:S(2)}) %collective-permute-start.22) | collective-permute-done | bytes 229408 | tf_op jit(solution)/shard_map/cond/branch_8_fun/ppermute | solution.py:286
  71.0 0.0 collective-permute-done.23.refs_3_
  71.0 1.5 %finish.27 = (bf16[2,48,2048]{2,1,0:T(8,128)(2,1)}, bf16[2,8,2048]{2,1,0:T(8,128)(2,1)}) custom-call(s32[10]{0:T(128)S(1)} %get-tuple-element.155.facts, bf16[2,16,56,128]{3,2,1,0:T(8,128)(2,1)S(1)} %bitcast.39, bf16[16,56,128]{2,1,0:T(8,128)(2,1)S(1)} %collective-permute-done.20.refs_0_, bf16[16,56,128]{2,1,0:T(8,128)(2,1)S(1)} %collective-permute-done.21.refs_1_, ...), custom_call_target="tpu_custom_call" | custom-call | tf_op jit(solution)/shard_map/cond/branch_8_fun/finish/pallas_call | solution.py:270
Async XLA Ops:
  29.9 19.2 %copy-start = (bf16[2,48,2048]{2,1,0:T(8,128)(2,1)S(1)}, bf16[2,48,2048]{2,1,0:T(8,128)(2,1)}, u32[]{:S(2)}) copy-start(bf16[2,48,2048]{2,1,0:T(8,128)(2,1)} %param.34) | copy-start | bytes 1179652
  34.7 14.4 %all-to-all-start.1 = ((bf16[32,56,128]{2,1,0:T(8,128)(2,1)}), bf16[32,56,128]{2,1,0:T(8,128)(2,1)S(1)}, u32[]{:S(2)}, u32[]{:S(2)}) async-start(bf16[32,56,128]{2,1,0:T(8,128)(2,1)} %attend.1._), calls=%async_computation.1 | async-start | bytes 917504 | tf_op jit(solution)/shard_map/all_to_all | solution.py:311
  49.7 7.2 %collective-permute-start.20 = (bf16[16,56,128]{2,1,0:T(8,128)(2,1)S(1)}, bf16[16,56,128]{2,1,0:T(8,128)(2,1)S(1)}, u32[]{:S(2)}, u32[]{:S(2)}) collective-permute-start(bf16[16,56,128]{2,1,0:T(8,128)(2,1)S(1)} %get-tuple-element.157), channel_id=1, source_target_pairs={{0,256},{1,257},{2,258},{3,259},{4,260},{5,261},{6,262},{7,263},{8... | collective-permute-start | bytes 688136 | tf_op jit(solution)/shard_map/cond/branch_8_fun/ppermute | solution.py:286
  50.4 16.0 %collective-permute-start.21 = (bf16[16,56,128]{2,1,0:T(8,128)(2,1)S(1)}, bf16[16,56,128]{2,1,0:T(8,128)(2,1)S(1)}, u32[]{:S(2)}, u32[]{:S(2)}) collective-permute-start(bf16[16,56,128]{2,1,0:T(8,128)(2,1)S(1)} %get-tuple-element.158), channel_id=1, source_target_pairs={{0,128},{128,384},{1,129},{129,385},{2,130},{130,386},{3,131},{131... | collective-permute-start | bytes 688136 | tf_op jit(solution)/shard_map/cond/branch_8_fun/ppermute | solution.py:286
  55.6 15.4 %collective-permute-start.22 = (bf16[16,56,128]{2,1,0:T(8,128)(2,1)S(1)}, bf16[16,56,128]{2,1,0:T(8,128)(2,1)S(1)}, u32[]{:S(2)}, u32[]{:S(2)}) collective-permute-start(bf16[16,56,128]{2,1,0:T(8,128)(2,1)S(1)} %get-tuple-element.159), channel_id=1, source_target_pairs={{0,128},{1,129},{2,130},{3,131},{4,132},{5,133},{6,134},{7,135},{8... | collective-permute-start | bytes 688136 | tf_op jit(solution)/shard_map/cond/branch_8_fun/ppermute | solution.py:286
  56.9 14.1 %collective-permute-start.23 = (bf16[16,56,128]{2,1,0:T(8,128)(2,1)S(1)}, bf16[16,56,128]{2,1,0:T(8,128)(2,1)S(1)}, u32[]{:S(2)}, u32[]{:S(2)}) collective-permute-start(bf16[16,56,128]{2,1,0:T(8,128)(2,1)S(1)} %collective-permute-done.20.refs_0_), channel_id=1, source_target_pairs={{256,384},{257,385},{258,386},{259,387},{260,388},{261,389},{262,3... | collective-permute-start | bytes 688136 | tf_op jit(solution)/shard_map/cond/branch_8_fun/ppermute | solution.py:293

commit v6 on v5

--- a/solution.py
+++ b/solution.py
@@ -90,42 +90,26 @@
     return [(key, arrange(*found[key]), found[key][1]) for key in sorted(found)]
 
 
-def pack_kernel(*refs, pieces):
-    arrays, out, held, sems = refs[:6], refs[6], refs[7:13], refs[13]
-    width = arrays[0].shape[2] // pieces
-
-    def copies(piece):
-        columns = pl.ds(piece * width, width)
-        return [
-            pltpu.make_async_copy(ref.at[:, :, columns], to.at[:, :, columns], sems.at[piece, i])
-            for i, (ref, to) in enumerate(zip(arrays, held))
-        ]
-
-    for piece in range(pieces):
-        for copy in copies(piece):
-            copy.start()
-    for piece in range(pieces):
-        for copy in copies(piece):
-            copy.wait()
-        for p in range(out.shape[0]):
-            for h in range(piece * width // HD, (piece + 1) * width // HD):
-                at = 0
-                for ref in held:
-                    out[p, h, at : at + ref.shape[1], :] = ref[p, :, h * HD : (h + 1) * HD]
-                    at += ref.shape[1]
-
-
-def pack(arrays, pieces=1):
+def pack_kernel(*refs):
+    arrays, out = refs[:-1], refs[-1]
+    for p in range(out.shape[0]):
+        for h in range(out.shape[1]):
+            at = 0
+            for ref in arrays:
+                out[p, h, at : at + ref.shape[1], :] = ref[p, :, h * HD : (h + 1) * HD]
+                at += ref.shape[1]
+
+
+def pack(arrays):
     resident, rows, features = arrays[0].shape
     text = arrays[3].shape[1]
     shape = (resident, features // HD, 3 * (rows + text), HD)
     packed = pl.pallas_call(
-        functools.partial(pack_kernel, pieces=pieces),
-        in_specs=[pl.BlockSpec(memory_space=pl.ANY)] * 6,
+        pack_kernel,
+        grid=(1,),
+        in_specs=[pl.BlockSpec(a.shape, lambda i: (0, 0, 0)) for a in arrays],
         out_specs=pl.BlockSpec(memory_space=pltpu.VMEM),
         out_shape=jax.ShapeDtypeStruct(shape, arrays[0].dtype),
-        scratch_shapes=[pltpu.VMEM(a.shape, a.dtype) for a in arrays]
-        + [pltpu.SemaphoreType.DMA((pieces, 6))],
         compiler_params=pltpu.CompilerParams(vmem_limit_bytes=SMALL),
         name="pack",
     )(*[pltpu.with_memory_space_constraint(a, pltpu.HBM) for a in arrays])

time: 72.8 us -> 71.8 us (0.986)
  the two profiles are of different devices: /device:TPU:160 before, /device:TPU:480 now
where the time goes in v6:
time: 71.8 us; the launch traced here: 71.5 us
  blocking collectives  27.8 us (39%)
  waiting for transfers between devices  25.7 us (36%)
  Pallas kernels  9.65 us (13%)
  starting transfers between devices  6.47 us (9%)
  between operations  1.31 us (2%)
    all_to_all x1, blocking collectives, per_device(): lax.all_to_all(packed, 'seq', split_axis=0, concat_axis=0, tiled=True)  27.8 us
    ppermute x2, waiting for transfers between devices, resample(): lax.ppermute(send, 'dom', [m[:2] for m in members])  17.8 us
    all_to_all x1, waiting for transfers between devices, per_device(): lax.all_to_all(attended, 'seq', split_axis=0, concat_axis=0, tiled=True)  7.93 us
    pallas_call x1, Pallas kernels, attend(): pl.pallas_call(functools.partial(attend_kernel, rows=rows, text=text, pee...  4.73 us
    all_to_all x1, starting transfers between devices, per_device(): lax.all_to_all(attended, 'seq', split_axis=0, concat_axis=0, tiled=True)  3.88 us
    ppermute x2, starting transfers between devices, resample(): lax.ppermute(send, 'dom', [m[:2] for m in members])  2.58 us
    pallas_call x1, Pallas kernels, pack(): pl.pallas_call(pack_kernel, grid=(1,), in_specs=[pl.BlockSpec(a.shape, la...  1.51 us
    pallas_call x1, Pallas kernels, finish(): pl.pallas_call(functools.partial(finish_kernel, places=places), in_specs=...  1.45 us
  transfers between devices with their start and end apart: 3, of which 3 were waited for; matrix products, arithmetic and copies ran while one was open for 1% of the time, Pallas kernels for 2%

profile of v6, /device:TPU:480, one launch (start us, length us, event | category | flops | bytes accessed | tf_op | source)
XLA Modules:
  0.0 71.5 jit_solution(941451750722520409)
XLA Ops:
  0.6 1.5 %pack.1 = bf16[2,16,168,128]{3,2,1,0:T(8,128)(2,1)S(1)} custom-call(bf16[2,48,2048]{2,1,0:T(8,128)(2,1)} %refs_0_.1, bf16[2,48,2048]{2,1,0:T(8,128)(2,1)} %refs_1_.1, bf16[2,48,2048]{2,1,0:T(8,128)(2,1)} %refs_2_.1, bf16[2,8,2048]{2,1,0:T(8,128)(2,1)} %refs_3_.1, bf16[2,8,2048]{2,1,0:T(8,128)(2,1)} %refs_4_.1, bf16[2,8,2048]{2,1,0:T(8,128)(2,1)} %refs_5_.1), custom_call_target="tpu_custom_call" | custom-call | tf_op jit(solution)/shard_map/pack/pallas_call | solution.py:107
  2.1 27.8 %all_to_all.10.x = bf16[32,168,128]{2,1,0:T(8,128)(2,1)S(1)} all-to-all(bf16[32,168,128]{2,1,0:T(8,128)(2,1)S(1)} %bitcast.21), channel_id=1, replica_groups=mesh['dom'=4,'seq'=32,'rep'=4] {'seq'}, dimensions={0} | all-to-all | bytes 2752512 | tf_op jit(solution)/shard_map/all_to_all | solution.py:292
  29.9 0.0 copy-start
  29.9 4.7 %attend.1._ = bf16[32,56,128]{2,1,0:T(8,128)(2,1)} custom-call(bf16[32,168,128]{2,1,0:T(8,128)(2,1)S(1)} %all_to_all.10.x), custom_call_target="tpu_custom_call" | custom-call | tf_op jit(solution)/shard_map/attend/pallas_call | solution.py:179
  34.6 3.9 %all-to-all-start.1 = ((bf16[32,56,128]{2,1,0:T(8,128)(2,1)}), bf16[32,56,128]{2,1,0:T(8,128)(2,1)S(1)}, u32[]{:S(2)}, u32[]{:S(2)}) async-start(bf16[32,56,128]{2,1,0:T(8,128)(2,1)} %attend.1._), calls=%async_computation.1 | async-start | bytes 917504 | tf_op jit(solution)/shard_map/all_to_all | solution.py:295
  38.5 1.4 %facts.1 = s32[10]{0:T(128)S(1)} custom-call(s32[8]{0:T(128)} %counts.1, bf16[32,56,128]{2,1,0:T(8,128)(2,1)} %attend.1._), custom_call_target="tpu_custom_call" | custom-call | tf_op jit(solution)/shard_map/facts/pallas_call | solution.py:134
  39.9 0.6 slice.3
  41.2 7.9 %all-to-all-done.1 = bf16[32,56,128]{2,1,0:T(8,128)(2,1)S(1)} async-done(((bf16[32,56,128]{2,1,0:T(8,128)(2,1)}), bf16[32,56,128]{2,1,0:T(8,128)(2,1)S(1)}, u32[]{:S(2)}, u32[]{:S(2)}) %all-to-all-start.1) | async-done | bytes 458784 | tf_op jit(solution)/shard_map/all_to_all | solution.py:295
  49.1 0.0 copy-done
  49.1 22.4 %conditional.1 = ((bf16[2,48,2048]{2,1,0:T(8,128)(2,1)}, bf16[2,8,2048]{2,1,0:T(8,128)(2,1)})) conditional(s32[]{:T(128)} %bitcast.20, (s32[10]{0:T(128)S(1)}, bf16[32,56,128]{2,1,0:T(8,128)(2,1)S(1)}, bf16[2,48,2048]{2,1,0:T(8,128)(2,1)S(1)}) %tuple.141, (s32[10]{0:T(128)S(1)}, bf16[32,56,128]{2,1,0:T(8,128)(2,1)S(1)}, ...), branch_computations={%region_0.0_spmd, %region_1.0_spmd, %region_2.0_spmd, %region_3.0_... | conditional | bytes 3670184 | solution.py:298
  49.1 0.6 outgoing.34
  49.7 1.3 %collective-permute-start.39 = (bf16[16,56,128]{2,1,0:T(8,128)(2,1)S(1)}, bf16[16,56,128]{2,1,0:T(8,128)(2,1)S(1)}, u32[]{:S(2)}, u32[]{:S(2)}) collective-permute-start(bf16[16,56,128]{2,1,0:T(8,128)(2,1)S(1)} %get-tuple-element.194), channel_id=1, source_target_pairs={{0,128},{128,256},{256,384},{1,129},{129,257},{257,385},{2,130},{1... | collective-permute-start | bytes 688136 | tf_op jit(solution)/shard_map/cond/branch_15_fun/ppermute | solution.py:270
  51.0 1.3 %collective-permute-start.40 = (bf16[16,56,128]{2,1,0:T(8,128)(2,1)S(1)}, bf16[16,56,128]{2,1,0:T(8,128)(2,1)S(1)}, u32[]{:S(2)}, u32[]{:S(2)}) collective-permute-start(bf16[16,56,128]{2,1,0:T(8,128)(2,1)S(1)} %get-tuple-element.195), channel_id=1, source_target_pairs={{0,256},{128,384},{1,257},{129,385},{2,258},{130,386},{3,259},{131... | collective-permute-start | bytes 688136 | tf_op jit(solution)/shard_map/cond/branch_15_fun/ppermute | solution.py:270
  52.3 7.5 %collective-permute-done.39.refs_0_ = bf16[16,56,128]{2,1,0:T(8,128)(2,1)S(1)} collective-permute-done((bf16[16,56,128]{2,1,0:T(8,128)(2,1)S(1)}, bf16[16,56,128]{2,1,0:T(8,128)(2,1)S(1)}, u32[]{:S(2)}, u32[]{:S(2)}) %collective-permute-start.39) | collective-permute-done | bytes 229408 | tf_op jit(solution)/shard_map/cond/branch_15_fun/ppermute | solution.py:270
  59.8 10.3 %collective-permute-done.40.refs_1_ = bf16[16,56,128]{2,1,0:T(8,128)(2,1)S(1)} collective-permute-done((bf16[16,56,128]{2,1,0:T(8,128)(2,1)S(1)}, bf16[16,56,128]{2,1,0:T(8,128)(2,1)S(1)}, u32[]{:S(2)}, u32[]{:S(2)}) %collective-permute-start.40) | collective-permute-done | bytes 229408 | tf_op jit(solution)/shard_map/cond/branch_15_fun/ppermute | solution.py:270
  70.1 1.5 %finish.34 = (bf16[2,48,2048]{2,1,0:T(8,128)(2,1)}, bf16[2,8,2048]{2,1,0:T(8,128)(2,1)}) custom-call(s32[10]{0:T(128)S(1)} %get-tuple-element.192.facts, bf16[2,16,56,128]{3,2,1,0:T(8,128)(2,1)S(1)} %bitcast.53, bf16[16,56,128]{2,1,0:T(8,128)(2,1)S(1)} %collective-permute-done.39.refs_0_, bf16[16,56,128]{2,1,0:T(8,128)(2,1)S(1)} %collective-permute-done.40.refs_1_, ...), custom_call_target="tpu_custom_call" | custom-call | tf_op jit(solution)/shard_map/cond/branch_15_fun/finish/pallas_call | solution.py:254
Async XLA Ops:
  29.9 19.2 %copy-start = (bf16[2,48,2048]{2,1,0:T(8,128)(2,1)S(1)}, bf16[2,48,2048]{2,1,0:T(8,128)(2,1)}, u32[]{:S(2)}) copy-start(bf16[2,48,2048]{2,1,0:T(8,128)(2,1)} %param.34) | copy-start | bytes 1179652
  34.6 14.4 %all-to-all-start.1 = ((bf16[32,56,128]{2,1,0:T(8,128)(2,1)}), bf16[32,56,128]{2,1,0:T(8,128)(2,1)S(1)}, u32[]{:S(2)}, u32[]{:S(2)}) async-start(bf16[32,56,128]{2,1,0:T(8,128)(2,1)} %attend.1._), calls=%async_computation.1 | async-start | bytes 917504 | tf_op jit(solution)/shard_map/all_to_all | solution.py:295
  49.7 10.1 %collective-permute-start.39 = (bf16[16,56,128]{2,1,0:T(8,128)(2,1)S(1)}, bf16[16,56,128]{2,1,0:T(8,128)(2,1)S(1)}, u32[]{:S(2)}, u32[]{:S(2)}) collective-permute-start(bf16[16,56,128]{2,1,0:T(8,128)(2,1)S(1)} %get-tuple-element.194), channel_id=1, source_target_pairs={{0,128},{128,256},{256,384},{1,129},{129,257},{257,385},{2,130},{1... | collective-permute-start | bytes 688136 | tf_op jit(solution)/shard_map/cond/branch_15_fun/ppermute | solution.py:270
  51.0 19.1 %collective-permute-start.40 = (bf16[16,56,128]{2,1,0:T(8,128)(2,1)S(1)}, bf16[16,56,128]{2,1,0:T(8,128)(2,1)S(1)}, u32[]{:S(2)}, u32[]{:S(2)}) collective-permute-start(bf16[16,56,128]{2,1,0:T(8,128)(2,1)S(1)} %get-tuple-element.195), channel_id=1, source_target_pairs={{0,256},{128,384},{1,257},{129,385},{2,258},{130,386},{3,259},{131... | collective-permute-start | bytes 688136 | tf_op jit(solution)/shard_map/cond/branch_15_fun/ppermute | solution.py:270

commit v7 on v6

--- a/solution.py
+++ b/solution.py
@@ -116,17 +116,27 @@
     return packed.reshape((-1,) + shape[2:])
 
 
-def facts_kernel(counts, _, facts, *, keys):
+def facts_kernel(counts, _, code, plan, *, keys):
     slots = counts.shape[0]
     running = [counts[0]]
     for i in range(1, slots):
         running.append(running[-1] + counts[i])
     row = [sum(jnp.where(r <= j, 1, 0) for r in running) for j in range(slots)]
-    facts[0] = lax.axis_index("dom")
+    dom = lax.axis_index("dom")
+    first, second = (
+        sum(jnp.where(dom == plane, row[2 * plane + s], 0) for plane in range(slots // 2))
+        for s in range(2)
+    )
+    kind = jnp.where(first // 2 == dom, lax.rem(first, 2), 2)
+    bits = dom + 4 * kind
+    kind = jnp.where(first == second, 3, 2)
+    kind = jnp.where(second // 2 == dom, lax.rem(second, 2), kind)
+    bits = bits + 16 * kind
     for j in range(slots):
-        facts[1 + j] = row[j]
+        bits = bits + lax.rem(row[j], 2) * 2 ** (6 + j)
+    code[...] = jnp.full(code.shape, bits, jnp.int32)
     key = key_of(row)
-    facts[1 + slots] = sum(jnp.where(key == k, i, 0) for i, k in enumerate(keys))
+    plan[0] = sum(jnp.where(key == k, i, 0) for i, k in enumerate(keys))
 
 
 def find_facts(counts, after, keys):
@@ -134,8 +144,11 @@
     return pl.pallas_call(
         functools.partial(facts_kernel, keys=keys),
         in_specs=[scalars, pl.BlockSpec(memory_space=pl.ANY)],
-        out_specs=scalars,
-        out_shape=jax.ShapeDtypeStruct((counts.shape[0] + 2,), jnp.int32),
+        out_specs=[pl.BlockSpec(memory_space=pltpu.VMEM), scalars],
+        out_shape=[
+            jax.ShapeDtypeStruct((8, HD), jnp.int32),
+            jax.ShapeDtypeStruct((1,), jnp.int32),
+        ],
         name="facts",
     )(counts, after)
 
@@ -191,11 +204,12 @@
 
 
 def outgoing_kernel(facts, own, *sends, rounds):
-    dom = facts[0]
+    bits = jnp.max(facts[...])
+    dom = bits & 3
     for members, send in zip(rounds, sends):
         index = 0
         for source, _, slot in members:
-            index = jnp.where(dom == source, lax.rem(facts[1 + slot], 2), index)
+            index = jnp.where(dom == source, (bits >> (6 + slot)) & 1, index)
         send[...] = own[index]
 
 
@@ -204,7 +218,7 @@
     block = jax.ShapeDtypeStruct(own.shape[1:], own.dtype)
     return pl.pallas_call(
         functools.partial(outgoing_kernel, rounds=rounds),
-        in_specs=[pl.BlockSpec(memory_space=pltpu.SMEM), vmem],
+        in_specs=[vmem, vmem],
         out_specs=[vmem] * len(rounds),
         out_shape=[block] * len(rounds),
         compiler_params=pltpu.CompilerParams(vmem_limit_bytes=SMALL),
@@ -216,18 +230,19 @@
     received, (noise, video, words) = refs[:-3], refs[-3:]
     slots, rows = noise.shape[0], noise.shape[1]
     text = words.shape[1]
-    dom = facts[0]
+    bits = jnp.max(facts[...])
+    dom = bits & 3
     chosen = 0
     for s in range(slots):
-        ancestor = facts[1 + slots * dom + s]
+        kind = (bits >> (2 + 2 * s)) & 3
         before = chosen
         chosen = 0
         for slot, r in places:
             if slot % slots == s:
                 chosen = jnp.where(dom == slot // slots, 1 + r, chosen)
         if s:
-            chosen = jnp.where(ancestor == facts[slots * dom + s], before, chosen)
-        chosen = jnp.where(ancestor // slots == dom, 0, chosen)
+            chosen = jnp.where(kind == 3, before, chosen)
+        chosen = jnp.where(kind < 2, 0, chosen)
 
         def write(block, s=s):
             for h in range(own.shape[1]):
@@ -238,8 +253,8 @@
                 words[s, :, columns] = block[h, rows : rows + text, :]
 
         @pl.when(chosen == 0)
-        def _(write=write, ancestor=ancestor):
-            write(own.at[lax.rem(ancestor, slots)])
+        def _(write=write, kind=kind):
+            write(own.at[kind & 1])
 
         for r, block in enumerate(received):
 
@@ -253,7 +268,7 @@
     vmem = pl.BlockSpec(memory_space=pltpu.VMEM)
     return pl.pallas_call(
         functools.partial(finish_kernel, places=places),
-        in_specs=[pl.BlockSpec(memory_space=pltpu.SMEM)] + [vmem] * (2 + len(received)),
+        in_specs=[vmem] * (3 + len(received)),
         out_specs=[vmem, vmem],
         out_shape=[
             jax.ShapeDtypeStruct(noise.shape, noise.dtype),
@@ -291,11 +306,11 @@
     )
     gathered = lax.all_to_all(packed, "seq", split_axis=0, concat_axis=0, tiled=True)
     attended = attend(gathered, rows, text)
-    facts = find_facts(counts, attended, [plan[0] for plan in known])
+    facts, plan = find_facts(counts, attended, [entry[0] for entry in known])
     returned = lax.all_to_all(attended, "seq", split_axis=0, concat_axis=0, tiled=True)
     own = returned.reshape(resident, heads, rows + text, HD)
-    branches = [functools.partial(resample, *plan[1:], text) for plan in known]
-    return lax.switch(facts[counts.shape[0] + 1], branches, facts, own, fresh_noise)
+    branches = [functools.partial(resample, *entry[1:], text) for entry in known]
+    return lax.switch(plan[0], branches, facts, own, fresh_noise)
 
 
 def solution(mesh):

time: 71.8 us -> 71.1 us (level)
  the two profiles are of different devices: /device:TPU:480 before, /device:TPU:353 now
where the time goes in v7:
time: 71.1 us; the launch traced here: 70.8 us
  blocking collectives  28.4 us (40%)
  waiting for transfers between devices  26.5 us (37%)
  Pallas kernels  8.88 us (12%)
  starting transfers between devices  5.64 us (8%)
  between operations  1.3 us (2%)
    all_to_all x1, blocking collectives, per_device(): lax.all_to_all(packed, 'seq', split_axis=0, concat_axis=0, tiled=True)  28.4 us
    ppermute x2, waiting for transfers between devices, resample(): lax.ppermute(send, 'dom', [m[:2] for m in members])  17.5 us
    all_to_all x1, waiting for transfers between devices, per_device(): lax.all_to_all(attended, 'seq', split_axis=0, concat_axis=0, tiled=True)  8.97 us
    pallas_call x1, Pallas kernels, attend(): pl.pallas_call(functools.partial(attend_kernel, rows=rows, text=text, pee...  4.73 us
    all_to_all x1, starting transfers between devices, per_device(): lax.all_to_all(attended, 'seq', split_axis=0, concat_axis=0, tiled=True)  3.67 us
    ppermute x2, starting transfers between devices, resample(): lax.ppermute(send, 'dom', [m[:2] for m in members])  1.97 us
    pallas_call x1, Pallas kernels, pack(): pl.pallas_call(pack_kernel, grid=(1,), in_specs=[pl.BlockSpec(a.shape, la...  1.51 us
  transfers between devices with their start and end apart: 3, of which 2 were waited for; matrix products, arithmetic and copies ran while one was open for 0% of the time, Pallas kernels for 2%

profile of v7, /device:TPU:353, one launch (start us, length us, event | category | flops | bytes accessed | tf_op | source)
XLA Modules:
  0.0 70.8 jit_solution(768123007558992932)
XLA Ops:
  0.6 1.5 %pack.1 = bf16[2,16,168,128]{3,2,1,0:T(8,128)(2,1)S(1)} custom-call(bf16[2,48,2048]{2,1,0:T(8,128)(2,1)} %refs_0_.1, bf16[2,48,2048]{2,1,0:T(8,128)(2,1)} %refs_1_.1, bf16[2,48,2048]{2,1,0:T(8,128)(2,1)} %refs_2_.1, bf16[2,8,2048]{2,1,0:T(8,128)(2,1)} %refs_3_.1, bf16[2,8,2048]{2,1,0:T(8,128)(2,1)} %refs_4_.1, bf16[2,8,2048]{2,1,0:T(8,128)(2,1)} %refs_5_.1), custom_call_target="tpu_custom_call" | custom-call | tf_op jit(solution)/shard_map/pack/pallas_call | solution.py:107
  2.1 28.4 %all_to_all.10.x = bf16[32,168,128]{2,1,0:T(8,128)(2,1)S(1)} all-to-all(bf16[32,168,128]{2,1,0:T(8,128)(2,1)S(1)} %bitcast.21), channel_id=1, replica_groups=mesh['dom'=4,'seq'=32,'rep'=4] {'seq'}, dimensions={0} | all-to-all | bytes 2752512 | tf_op jit(solution)/shard_map/all_to_all | solution.py:307
  30.6 0.0 copy-start
  30.6 4.7 %attend.1._ = bf16[32,56,128]{2,1,0:T(8,128)(2,1)} custom-call(bf16[32,168,128]{2,1,0:T(8,128)(2,1)S(1)} %all_to_all.10.x), custom_call_target="tpu_custom_call" | custom-call | tf_op jit(solution)/shard_map/attend/pallas_call | solution.py:192
  35.3 3.7 %all-to-all-start.1 = ((bf16[32,56,128]{2,1,0:T(8,128)(2,1)}), bf16[32,56,128]{2,1,0:T(8,128)(2,1)S(1)}, u32[]{:S(2)}, u32[]{:S(2)}) async-start(bf16[32,56,128]{2,1,0:T(8,128)(2,1)} %attend.1._), calls=%async_computation.1 | async-start | bytes 917504 | tf_op jit(solution)/shard_map/all_to_all | solution.py:310
  39.0 1.3 %facts.1 = (s32[8,128]{1,0:T(8,128)S(1)}, s32[1]{0:T(128)}) custom-call(s32[8]{0:T(128)} %counts.1, bf16[32,56,128]{2,1,0:T(8,128)(2,1)} %attend.1._), custom_call_target="tpu_custom_call" | custom-call | tf_op jit(solution)/shard_map/facts/pallas_call | solution.py:144
  41.0 9.0 %all-to-all-done.1 = bf16[32,56,128]{2,1,0:T(8,128)(2,1)S(1)} async-done(((bf16[32,56,128]{2,1,0:T(8,128)(2,1)}), bf16[32,56,128]{2,1,0:T(8,128)(2,1)S(1)}, u32[]{:S(2)}, u32[]{:S(2)}) %all-to-all-start.1) | async-done | bytes 458784 | tf_op jit(solution)/shard_map/all_to_all | solution.py:310
  49.9 0.0 copy-done
  49.9 20.8 %conditional.1 = ((bf16[2,48,2048]{2,1,0:T(8,128)(2,1)}, bf16[2,8,2048]{2,1,0:T(8,128)(2,1)})) conditional(s32[]{:T(128)} %bitcast.20, (s32[8,128]{1,0:T(8,128)S(1)}, bf16[32,56,128]{2,1,0:T(8,128)(2,1)S(1)}, bf16[2,48,2048]{2,1,0:T(8,128)(2,1)S(1)}) %tuple.141, (s32[8,128]{1,0:T(8,128)S(1)}, ...), branch_computations={%region_0.0_spmd, %region_1.0_spmd, %region_2.0_spmd, %region_3.0_... | conditional | bytes 3670184 | solution.py:313
  49.9 0.2 outgoing.25
  50.2 0.7 collective-permute-start.15
  50.9 1.3 %collective-permute-start.16 = (bf16[16,56,128]{2,1,0:T(8,128)(2,1)S(1)}, bf16[16,56,128]{2,1,0:T(8,128)(2,1)S(1)}, u32[]{:S(2)}, u32[]{:S(2)}) collective-permute-start(bf16[16,56,128]{2,1,0:T(8,128)(2,1)S(1)} %get-tuple-element.148), channel_id=1, source_target_pairs={{0,256},{128,384},{1,257},{129,385},{2,258},{130,386},{3,259},{131... | collective-permute-start | bytes 688136 | tf_op jit(solution)/shard_map/cond/branch_6_fun/ppermute | solution.py:285
  52.2 0.0 collective-permute-done.15.refs_0_
  52.2 17.5 %collective-permute-done.16.refs_1_ = bf16[16,56,128]{2,1,0:T(8,128)(2,1)S(1)} collective-permute-done((bf16[16,56,128]{2,1,0:T(8,128)(2,1)S(1)}, bf16[16,56,128]{2,1,0:T(8,128)(2,1)S(1)}, u32[]{:S(2)}, u32[]{:S(2)}) %collective-permute-start.16) | collective-permute-done | bytes 229408 | tf_op jit(solution)/shard_map/cond/branch_6_fun/ppermute | solution.py:285
  69.7 1.1 %finish.25 = (bf16[2,48,2048]{2,1,0:T(8,128)(2,1)}, bf16[2,8,2048]{2,1,0:T(8,128)(2,1)}) custom-call(s32[8,128]{1,0:T(8,128)S(1)} %get-tuple-element.145.facts, bf16[2,16,56,128]{3,2,1,0:T(8,128)(2,1)S(1)} %bitcast.35, bf16[16,56,128]{2,1,0:T(8,128)(2,1)S(1)} %collective-permute-done.15.refs_0_, bf16[16,56,128]{2,1,0:T(8,128)(2,1)S(1)} %collective-permute-done.16.refs_1_, ...), custom_call_target="tpu_custom_call" | custom-call | tf_op jit(solution)/shard_map/cond/branch_6_fun/finish/pallas_call | solution.py:269
Async XLA Ops:
  30.6 19.4 %copy-start = (bf16[2,48,2048]{2,1,0:T(8,128)(2,1)S(1)}, bf16[2,48,2048]{2,1,0:T(8,128)(2,1)}, u32[]{:S(2)}) copy-start(bf16[2,48,2048]{2,1,0:T(8,128)(2,1)} %param.34) | copy-start | bytes 1179652
  35.3 14.6 %all-to-all-start.1 = ((bf16[32,56,128]{2,1,0:T(8,128)(2,1)}), bf16[32,56,128]{2,1,0:T(8,128)(2,1)S(1)}, u32[]{:S(2)}, u32[]{:S(2)}) async-start(bf16[32,56,128]{2,1,0:T(8,128)(2,1)} %attend.1._), calls=%async_computation.1 | async-start | bytes 917504 | tf_op jit(solution)/shard_map/all_to_all | solution.py:310
  50.2 2.0 %collective-permute-start.15 = (bf16[16,56,128]{2,1,0:T(8,128)(2,1)S(1)}, bf16[16,56,128]{2,1,0:T(8,128)(2,1)S(1)}, u32[]{:S(2)}, u32[]{:S(2)}) collective-permute-start(bf16[16,56,128]{2,1,0:T(8,128)(2,1)S(1)} %get-tuple-element.147), channel_id=1, source_target_pairs={{0,128},{128,256},{1,129},{129,257},{2,130},{130,258},{3,131},{131... | collective-permute-start | bytes 688136 | tf_op jit(solution)/shard_map/cond/branch_6_fun/ppermute | solution.py:285
  50.9 18.8 %collective-permute-start.16 = (bf16[16,56,128]{2,1,0:T(8,128)(2,1)S(1)}, bf16[16,56,128]{2,1,0:T(8,128)(2,1)S(1)}, u32[]{:S(2)}, u32[]{:S(2)}) collective-permute-start(bf16[16,56,128]{2,1,0:T(8,128)(2,1)S(1)} %get-tuple-element.148), channel_id=1, source_target_pairs={{0,256},{128,384},{1,257},{129,385},{2,258},{130,386},{3,259},{131... | collective-permute-start | bytes 688136 | tf_op jit(solution)/shard_map/cond/branch_6_fun/ppermute | solution.py:285
